TPU v7x, 128 devices: a whole 4x4x4 slice. The times are simulated.
128 devices in a mesh: grp: 8 (over z, core), ctx: 16 (over x, y).
Axes of the slice: x: 4, y: 4, z: 4, core: 2. Of those that a mesh axis runs over, the one named last changes fastest.
Arguments:
- index_query: bfloat16 [256, 8192], P(('grp', 'ctx')), may hold values from -6 to 6
- index_weights: bfloat16 [256, 64], P(('grp', 'ctx')), may hold values from -0.125 to 0.125
- index_keys: bfloat16 [1048576, 128], P(('grp', 'ctx')), may hold values from -6 to 6
- key_scales: float32 [1048576], P(('grp', 'ctx')), may hold values from 0.25 to 4
- attn_query: bfloat16 [256, 128, 576], P(('grp', 'ctx')), may hold values from -360 to 360
- compact_cache: bfloat16 [1048576, 576], P(('grp', 'ctx')), may hold values from -6 to 6
- top_pos: int32 [256, 16, 256], P(('grp', 'ctx')), may hold values from 0 to 8191, as said below
- owner_counts: int32 [256, 16], P(('grp', 'ctx')), may hold values from 1 to 256, 2048 in all within a row
- moe_input: bfloat16 [256, 7168], P(('grp', 'ctx')), may hold values from -6 to 6
- expert_ids: int32 [256, 8], P(('grp', 'ctx')), may hold values from 0 to 15, all different within a row
- expert_gates: float32 [256, 8], P(('grp', 'ctx')), may hold values from 0.05 to 0.5
- gate_proj: bfloat16 [16, 7168, 2048], P('grp', None, 'ctx'), may hold values from -0.0625 to 0.0625
- up_proj: bfloat16 [16, 7168, 2048], P('grp', None, 'ctx'), may hold values from -0.0625 to 0.0625
- down_proj: bfloat16 [16, 2048, 7168], P('grp', 'ctx'), may hold values from -0.125 to 0.125
Outputs:
- index_scores: float32 [256, 131072], P('grp', 'ctx')
- attn_out: bfloat16 [256, 128, 512], P(('grp', 'ctx'))
- moe_out: bfloat16 [256, 7168], P(('grp', 'ctx'))
Inputs may be any that keep to these rules, and one draw needn't show every extreme that they name: `top_pos`: for each sample row and device, the first owner_counts slots hold distinct positions; later slots hold arbitrary positions. `owner_counts`: each sample row's counts sum to 2048, and some device holds exactly 256 of them. `expert_ids`: each row names 8 different experts.
All inputs are finite; a program needn't handle non-finite values.
Results may differ from a plain program's by a relative error of at most 0.014.
Values may be sent and summed in bfloat16 or wider, within the bound.
A program may use at most 256 MiB of HBM per device.

v0:
```python
import jax
import jax.numpy as jnp
from jax import lax
from jax.sharding import PartitionSpec as P

LATENT_RANK = 512
IHEADS = 64
IDIM = 128


score_scale = 192.0 ** (-0.5)


def expert_apply(tokens, gate_local, up_local, down_local):
    gate_part = jnp.einsum("egrd,edf->egrf", tokens, gate_local, preferred_element_type=jnp.float32)
    up_part = jnp.einsum("egrd,edf->egrf", tokens, up_local, preferred_element_type=jnp.float32)
    hidden = (jax.nn.silu(gate_part) * up_part).astype(jnp.bfloat16)
    return jnp.einsum("egrf,efd->egrd", hidden, down_local, preferred_element_type=jnp.float32)


def local(
    index_query,
    index_weights,
    index_keys,
    key_scales,
    attn_query,
    compact_cache,
    top_pos,
    owner_counts,
    moe_input,
    expert_ids,
    expert_gates,
    gate_proj,
    up_proj,
    down_proj,
):
    ctx_count = lax.axis_size("ctx")
    grp_count = lax.axis_size("grp")
    rows_dev = index_query.shape[0]
    cache_rows = index_keys.shape[0]
    latent_width = compact_cache.shape[1]
    queries, head_weights = (
        lax.all_gather(index_query, "ctx", axis=0, tiled=True),
        lax.all_gather(index_weights, "ctx", axis=0, tiled=True),
    )
    group_rows = queries.shape[0]
    products = jnp.dot(
        queries.reshape(group_rows * IHEADS, IDIM), index_keys.T, preferred_element_type=jnp.float32
    )
    active = jnp.maximum(products, 0.0).reshape(group_rows, IHEADS, cache_rows)
    index_scores = (
        jnp.einsum("rhs,rh->rs", active, head_weights.astype(jnp.float32)) * key_scales[None, :]
    )
    capacity = top_pos.shape[2]
    slot_index = jnp.arange(capacity, dtype=jnp.int32)
    requested = lax.all_to_all(top_pos, "ctx", split_axis=1, concat_axis=1, tiled=True)
    served = jnp.take(compact_cache, requested.reshape(-1), axis=0).reshape(
        rows_dev, ctx_count, capacity, latent_width
    )
    loaded_rows = lax.all_to_all(served, "ctx", split_axis=1, concat_axis=1, tiled=True).reshape(
        rows_dev, ctx_count * capacity, latent_width
    )
    live_slot = (slot_index[None, None, :] < owner_counts[:, :, None]).reshape(
        rows_dev, 1, ctx_count * capacity
    )
    scores = (
        jnp.einsum("rhd,rsd->rhs", attn_query, loaded_rows, preferred_element_type=jnp.float32)
        * score_scale
    )
    row_peak = jnp.max(jnp.where(live_slot, scores, -1e30), axis=2, keepdims=True)
    exponent = jnp.where(live_slot, jnp.exp(scores - row_peak), 0.0)
    denominator = jnp.sum(exponent, axis=2)
    softmax_weights = exponent.astype(jnp.bfloat16)
    weighted_total = jnp.einsum(
        "zlv,zvt->zlt",
        softmax_weights,
        loaded_rows[:, :, :LATENT_RANK],
        preferred_element_type=jnp.float32,
    )
    attn_out = (weighted_total / denominator[:, :, None]).astype(jnp.bfloat16)
    experts_dev = gate_proj.shape[0]
    model_width = moe_input.shape[1]
    expert_grid = (
        jnp.arange(experts_dev, dtype=jnp.int32)[:, None]
        + experts_dev * jnp.arange(grp_count, dtype=jnp.int32)[None, :]
    )
    matches = expert_ids[:, :, None, None] == expert_grid[None, None, :, :]
    chosen = jnp.any(matches, axis=1)
    gate_table = jnp.sum(expert_gates[:, :, None, None] * matches.astype(jnp.float32), axis=1)
    routed = jnp.where(
        jnp.transpose(chosen, (1, 2, 0))[:, :, :, None],
        moe_input[None, None, :, :],
        jnp.zeros_like(moe_input)[None, None, :, :],
    )
    copies = jnp.broadcast_to(
        routed[:, :, None], (experts_dev, grp_count, ctx_count, rows_dev, model_width)
    ).reshape(experts_dev, grp_count * ctx_count, rows_dev, model_width)
    arrived = lax.all_to_all(
        copies, ("grp", "ctx"), split_axis=1, concat_axis=1, tiled=True
    ).reshape(experts_dev, grp_count, ctx_count * rows_dev, model_width)
    shard_terms = expert_apply(arrived, gate_proj, up_proj, down_proj).reshape(
        experts_dev, grp_count * ctx_count, rows_dev, model_width
    )
    returned = (
        lax.all_to_all(shard_terms, ("grp", "ctx"), split_axis=1, concat_axis=1, tiled=True)
        .reshape(experts_dev, grp_count, ctx_count, rows_dev, model_width)
        .sum(axis=2)
    )
    moe_out = jnp.einsum("reg,egrd->rd", gate_table, returned).astype(jnp.bfloat16)
    return (index_scores, attn_out, moe_out)


def solution(mesh):
    in_specs = (
        P(("grp", "ctx"), None),
        P(("grp", "ctx"), None),
        P(("grp", "ctx"), None),
        P(("grp", "ctx")),
        P(("grp", "ctx"), None, None),
        P(("grp", "ctx"), None),
        P(("grp", "ctx"), None, None),
        P(("grp", "ctx"), None),
        P(("grp", "ctx"), None),
        P(("grp", "ctx"), None),
        P(("grp", "ctx"), None),
        P("grp", None, "ctx"),
        P("grp", None, "ctx"),
        P("grp", "ctx", None),
    )
    out_specs = (P("grp", "ctx"), P(("grp", "ctx"), None, None), P(("grp", "ctx"), None))
    return jax.shard_map(local, mesh=mesh, in_specs=in_specs, out_specs=out_specs, check_vma=False)
```

profile of v0, /device:TPU:0, one launch (start us, length us, event | category | flops | bytes accessed | tf_op | source)
XLA Modules:
  0.0 607.3 jit_solution(1354262189925107610)
XLA Ops:
  0.6 0.0 copy-start
  0.6 1.5 copy.47
  2.2 7.1 %all-to-all-start = ((s32[2,16,256]{2,0,1:T(2,128)}), s32[2,16,256]{2,0,1:T(2,128)S(1)}, u32[]{:S(2)}, u32[]{:S(2)}) async-start(s32[2,16,256]{2,0,1:T(2,128)} %copy.47), calls=%async_computation | async-start | bytes 65536 | tf_op jit(solution)/shard_map/all_to_all | solution.py:56
  9.3 0.8 compare_reduce_fusion
  10.1 0.1 copy.54
  10.2 1.1 broadcast_select_fusion.1
  11.4 5.6 all-to-all-done
  16.9 5.3 broadcast_in_dim.78
  22.2 7.8 %all-to-all-start.2 = ((bf16[2,128,2,7168]{3,2,0,1:T(2,128)(2,1)}), bf16[2,128,2,7168]{3,2,0,1:T(2,128)(2,1)}, u32[]{:S(2)}, u32[]{:S(2)}) async-start(bf16[2,128,2,7168]{3,2,0,1:T(2,128)(2,1)} %bitcast.68), calls=%async_computation.2 | async-start | bytes 14680064 | tf_op jit(solution)/shard_map/all_to_all | solution.py:98
  30.0 14.1 %copy.49 = bf16[8192,576]{1,0:T(8,128)(2,1)} copy(bf16[8192,576]{0,1:T(8,128)(2,1)} %param.19) | data formatting | bytes 18874368 | tf_op args[5]
  44.2 40.4 %gather_fusion = bf16[8192,576]{1,0:T(8,128)(2,1)} fusion(bf16[8192,576]{1,0:T(8,128)(2,1)} %copy.49, s32[8192]{0:T(1024)S(1)} %broadcast_clamp_fusion), kind=kCustom, calls=%fused_computation | custom fusion | bytes 18907136 | tf_op jit(solution)/shard_map/jit(_take)/gather | solution.py:57
  84.6 14.6 %copy.50 = bf16[2,16,256,576]{2,3,0,1:T(8,128)(2,1)} copy(bf16[2,16,256,576]{3,2,1,0:T(8,128)(2,1)} %bitcast.63) | data formatting | bytes 18874368 | tf_op jit(solution)/shard_map/jit(_take)/gather | solution.py:57
  99.2 8.1 %broadcast_select_fusion = bf16[2,16,256,576]{2,3,0,1:T(8,128)(2,1)} fusion(bf16[2,16,256,576]{2,3,0,1:T(8,128)(2,1)} %copy.50, pred[2,16,256]{2,0,1:T(4,128)(4,1)S(1)} %compare_and_fusion), kind=kLoop, calls=%fused_computation.4 | loop fusion | flops 4718592 | bytes 18882560 | tf_op jit(solution)/shard_map/jit(_take)/select_n | solution.py:57
  107.3 8.9 %all-to-all-done.2 = bf16[2,128,2,7168]{3,2,0,1:T(2,128)(2,1)} async-done(((bf16[2,128,2,7168]{3,2,0,1:T(2,128)(2,1)}), bf16[2,128,2,7168]{3,2,0,1:T(2,128)(2,1)}, u32[]{:S(2)}, u32[]{:S(2)}) %all-to-all-start.2) | async-done | bytes 7340064 | tf_op jit(solution)/shard_map/all_to_all | solution.py:98
  116.2 7.3 %all-to-all-start.1 = ((bf16[2,16,256,576]{2,3,0,1:T(8,128)(2,1)}), bf16[2,16,256,576]{2,3,0,1:T(8,128)(2,1)}, u32[]{:S(2)}, u32[]{:S(2)}) async-start(bf16[2,16,256,576]{2,3,0,1:T(8,128)(2,1)} %broadcast_select_fusion), calls=%async_computation.1 | async-start | bytes 18874368 | tf_op jit(solution)/shard_map/all_to_all | solution.py:60
  123.5 7.3 %copy.55 = bf16[2,128,2,7168]{3,2,1,0:T(2,128)(2,1)} copy(bf16[2,128,2,7168]{3,2,0,1:T(2,128)(2,1)} %all-to-all-done.2) | data formatting | bytes 14680064 | tf_op jit(solution)/shard_map/all_to_all | solution.py:98
  130.8 15.4 %reshape.125 = bf16[2,8,32,7168]{3,2,1,0:T(8,128)(2,1)} reshape(bf16[2,128,2,7168]{3,2,1,0:T(2,128)(2,1)} %copy.55) | data formatting | bytes 14680064 | tf_op jit(solution)/shard_map/reshape | solution.py:100
  146.2 6.2 %fusion.18 = f32[2,8,32,128]{3,2,1,0:T(8,128)S(1)} fusion(bf16[2,8,32,7168]{3,2,1,0:T(8,128)(2,1)} %reshape.125, bf16[2,7168,128]{2,1,0:T(8,128)(2,1)} %param.25), kind=kOutput, calls=%fused_computation.18 | convolution fusion | flops 939524096 | bytes 11272192 | tf_op jit(solution)/shard_map/egrd,edf->egrf/dot_general | solution.py:15
  152.4 14.4 %fusion.14 = f32[2,8,32,7168]{3,2,1,0:T(8,128)} fusion(bf16[2,128,7168]{2,1,0:T(8,128)(2,1)} %param.27, bf16[2,8,32,7168]{3,2,1,0:T(8,128)(2,1)} %reshape.125, bf16[2,7168,128]{2,1,0:T(8,128)(2,1)} %param.26, f32[2,8,32,128]{3,2,1,0:T(8,128)S(1)} %fusion.18), kind=kOutput, calls=%fused_computation.14 | convolution fusion | flops 1879441408 | bytes 29622272 | tf_op jit(solution)/shard_map/egrf,efd->egrd/dot_general | solution.py:18
  166.9 17.3 %reshape.126 = f32[2,128,2,7168]{3,2,1,0:T(2,128)} reshape(f32[2,8,32,7168]{3,2,1,0:T(8,128)} %fusion.14) | data formatting | bytes 29360128 | tf_op jit(solution)/shard_map/reshape | solution.py:101
  184.1 10.9 %copy.56 = f32[2,128,2,7168]{3,2,0,1:T(2,128)} copy(f32[2,128,2,7168]{3,2,1,0:T(2,128)} %reshape.126) | data formatting | bytes 29360128 | tf_op jit(solution)/shard_map/reshape | solution.py:101
  195.0 0.0 copy-start.7
  195.0 0.0 copy-start.4
  195.1 0.0 copy-start.6
  195.1 92.1 %all-to-all-done.1 = bf16[2,16,256,576]{2,3,0,1:T(8,128)(2,1)} async-done(((bf16[2,16,256,576]{2,3,0,1:T(8,128)(2,1)}), bf16[2,16,256,576]{2,3,0,1:T(8,128)(2,1)}, u32[]{:S(2)}, u32[]{:S(2)}) %all-to-all-start.1) | async-done | bytes 9437216 | tf_op jit(solution)/shard_map/all_to_all | solution.py:60
  287.2 14.8 %all-to-all-start.3 = ((f32[2,128,2,7168]{3,2,0,1:T(2,128)}), f32[2,128,2,7168]{3,2,0,1:T(2,128)}, u32[]{:S(2)}, u32[]{:S(2)}) async-start(f32[2,128,2,7168]{3,2,0,1:T(2,128)} %copy.56), calls=%async_computation.3 | async-start | bytes 29360128 | tf_op jit(solution)/shard_map/all_to_all | solution.py:105
  301.9 0.0 copy-done.3
  302.0 229.3 %all-gather = bf16[16,2,8192]{2,1,0:T(2,128)(2,1)S(1)} all-gather(bf16[1,2,8192]{2,1,0:T(2,128)(2,1)S(1)} %bitcast.73), channel_id=1, replica_groups=mesh['grp'=8,'ctx'=16] {'ctx'}, dimensions={0}, use_global_device_ids=true | all-gather | bytes 557056 | tf_op jit(solution)/shard_map/all_gather | solution.py:43
  531.2 0.4 reshape.120
  531.6 0.0 copy-done.5
  531.6 0.1 broadcast_bitcast_fusion
  531.8 0.0 copy-done.7
  531.8 18.2 %all-gather.1 = bf16[16,2,64]{2,1,0:T(2,128)(2,1)S(1)} all-gather(bf16[1,2,64]{2,1,0:T(2,128)(2,1)S(1)} %bitcast.77), channel_id=1, replica_groups=mesh['grp'=8,'ctx'=16] {'ctx'}, dimensions={0}, use_global_device_ids=true | all-gather | bytes 4352 | tf_op jit(solution)/shard_map/all_gather | solution.py:44
  549.9 0.0 copy-done.4
  550.0 0.1 fusion.49
  550.1 14.7 %broadcast_maximum_fusion = bf16[2048,8192]{1,0:T(8,128)(2,1)} fusion(bf16[2048,128]{1,0:T(8,128)(2,1)S(1)} %reshape.120, bf16[8192,128]{1,0:T(8,128)(2,1)S(1)} %copy-done), kind=kOutput, calls=%fused_computation.2 | convolution fusion | flops 4328521728 | bytes 36175872 | tf_op jit(solution)/shard_map/dot_general | solution.py:47
  564.8 12.4 %fusion.50 = f32[32,1,8192]{2,1,0:T(1,128)S(1)} fusion(bf16[32,64,8192]{2,1,0:T(8,128)(2,1)} %bitcast.62, bf16[32,64,1]{1,0,2:T(8,128)(2,1)S(1)} %bitcast.71), kind=kOutput, calls=%fused_computation.45 | convolution fusion | flops 33554432 | bytes 34607104 | tf_op jit(solution)/shard_map/rhs,rh->rs/dot_general | solution.py:52
  577.2 0.0 copy-done.2
  577.2 1.6 bitcast_multiply_fusion
  578.8 8.7 %copy.67 = bf16[16,2,72,8,256]{4,3,0,2,1:T(8,128)(2,1)} copy(bf16[16,2,72,8,256]{4,3,2,1,0:T(8,128)(2,1)} %bitcast.26) | data formatting | bytes 18874368 | tf_op jit(solution)/shard_map/reshape | solution.py:60
  587.5 6.5 %convolution_multiply_fusion = f32[2,4096,128]{2,1,0:T(8,128)S(1)} fusion(bf16[2,4096,576]{1,2,0:T(8,128)(2,1)} %bitcast.64, bf16[2,128,576]{1,2,0:T(8,128)(2,1)S(1)} %copy-done.1), kind=kOutput, calls=%fused_computation.11 | convolution fusion | flops 1209008128 | bytes 13926400 | tf_op jit(solution)/shard_map/rhd,rsd->rhs/dot_general | solution.py:67
  594.0 0.0 slice-start.2
  594.0 2.4 fusion.54
  596.4 3.6 fusion.36
  600.0 0.0 all-to-all-done.3
  600.0 6.3 %bitcast_reduce_fusion = bf16[2,8,2,7168]{3,2,0,1:T(2,128)(2,1)S(1)} fusion(f32[2,128,2,7168]{3,2,0,1:T(2,128)} %all-to-all-done.3), kind=kLoop, calls=%fused_computation.3 | loop fusion | flops 3440640 | bytes 15138816 | tf_op jit(solution)/shard_map/reduce_sum | solution.py:107
  606.3 0.4 fusion.41
  606.7 0.6 copy.76
  (24 shorter events, 0.2 us)
Async XLA Ops:
  0.6 549.4 %copy-start = (bf16[8192,128]{1,0:T(8,128)(2,1)S(1)}, bf16[8192,128]{1,0:T(8,128)(2,1)}, u32[]{:S(2)}) copy-start(bf16[8192,128]{1,0:T(8,128)(2,1)} %param.16) | copy-start | bytes 6291460
  2.2 14.7 %all-to-all-start = ((s32[2,16,256]{2,0,1:T(2,128)}), s32[2,16,256]{2,0,1:T(2,128)S(1)}, u32[]{:S(2)}, u32[]{:S(2)}) async-start(s32[2,16,256]{2,0,1:T(2,128)} %copy.47), calls=%async_computation | async-start | bytes 65536 | tf_op jit(solution)/shard_map/all_to_all | solution.py:56
  22.2 94.0 %all-to-all-start.2 = ((bf16[2,128,2,7168]{3,2,0,1:T(2,128)(2,1)}), bf16[2,128,2,7168]{3,2,0,1:T(2,128)(2,1)}, u32[]{:S(2)}, u32[]{:S(2)}) async-start(bf16[2,128,2,7168]{3,2,0,1:T(2,128)(2,1)} %bitcast.68), calls=%async_computation.2 | async-start | bytes 14680064 | tf_op jit(solution)/shard_map/all_to_all | solution.py:98
  116.2 171.0 %all-to-all-start.1 = ((bf16[2,16,256,576]{2,3,0,1:T(8,128)(2,1)}), bf16[2,16,256,576]{2,3,0,1:T(8,128)(2,1)}, u32[]{:S(2)}, u32[]{:S(2)}) async-start(bf16[2,16,256,576]{2,3,0,1:T(8,128)(2,1)} %broadcast_select_fusion), calls=%async_computation.1 | async-start | bytes 18874368 | tf_op jit(solution)/shard_map/all_to_all | solution.py:60
  195.0 106.9 %copy-start.3 = (bf16[2,8192]{1,0:T(2,128)(2,1)S(1)}, bf16[2,8192]{1,0:T(2,128)(2,1)}, u32[]{:S(2)}) copy-start(bf16[2,8192]{1,0:T(2,128)(2,1)} %param.14) | copy-start | bytes 98308
  195.0 336.6 %copy-start.5 = (s32[2,16]{1,0:T(2,128)S(1)}, s32[2,16]{1,0:T(2,128)}, u32[]{:S(2)}) copy-start(s32[2,16]{1,0:T(2,128)} %param.21) | copy-start | bytes 388
  195.0 336.7 %copy-start.7 = (bf16[2,64]{1,0:T(2,128)(2,1)S(1)}, bf16[2,64]{1,0:T(2,128)(2,1)}, u32[]{:S(2)}) copy-start(bf16[2,64]{1,0:T(2,128)(2,1)} %param.15) | copy-start | bytes 772
  195.0 354.9 %copy-start.4 = (s32[2,8]{1,0:T(2,128)S(1)}, s32[2,8]{1,0:T(2,128)}, u32[]{:S(2)}) copy-start(s32[2,8]{1,0:T(2,128)} %param.23) | copy-start | bytes 196
  195.1 354.9 %copy-start.6 = (f32[2,8]{1,0:T(2,128)S(1)}, f32[2,8]{1,0:T(2,128)}, u32[]{:S(2)}) copy-start(f32[2,8]{1,0:T(2,128)} %param.24) | copy-start | bytes 196
  287.2 312.8 %all-to-all-start.3 = ((f32[2,128,2,7168]{3,2,0,1:T(2,128)}), f32[2,128,2,7168]{3,2,0,1:T(2,128)}, u32[]{:S(2)}, u32[]{:S(2)}) async-start(f32[2,128,2,7168]{3,2,0,1:T(2,128)} %copy.56), calls=%async_computation.3 | async-start | bytes 29360128 | tf_op jit(solution)/shard_map/all_to_all | solution.py:105
  564.8 12.4 %copy-start.2 = (f32[8192]{0:T(1024)S(1)}, f32[8192]{0:T(1024)}, u32[]{:S(2)}) copy-start(f32[8192]{0:T(1024)} %param.17) | copy-start | bytes 98308
  578.8 8.7 %copy-start.1 = (bf16[2,128,576]{1,2,0:T(8,128)(2,1)S(1)}, bf16[2,128,576]{1,2,0:T(8,128)(2,1)}, u32[]{:S(2)}) copy-start(bf16[2,128,576]{1,2,0:T(8,128)(2,1)} %param.18) | copy-start | bytes 884740
  587.5 8.9 %slice-start = ((s8[9437184]{0:T(1024)(128)(4,1)}), s8[1048576]{0:T(1024)(128)(4,1)S(1)}, s32[]{:S(2)}) async-start(s8[9437184]{0:T(1024)(128)(4,1)} %bitcast.65), calls=%async_computation.4 | async-start | bytes 2097152
  587.5 8.9 %slice-start.1 = ((s8[9437184]{0:T(1024)(128)(4,1)}), s8[4194304]{0:T(1024)(128)(4,1)S(1)}, s32[]{:S(2)}) async-start(s8[9437184]{0:T(1024)(128)(4,1)} %bitcast.65), calls=%async_computation.5 | async-start | bytes 8388608
  594.0 2.4 slice-start.2
where the time goes:
time: 610 us; the launch traced here: 607 us
  blocking collectives  247 us (40%)
  local copies, waits for them, and re-layouts  137 us (22%)
  waiting for transfers between devices  107 us (18%)
  matrix products  58.1 us (10%)
  starting transfers between devices  36.9 us (6%)
  other arithmetic  20.5 us (3%)
    all_gather x1, blocking collectives, local(): lax.all_gather(index_query, 'ctx', axis=0, tiled=True)  229 us
    all_to_all x1, waiting for transfers between devices, local(): lax.all_to_all(served, 'ctx', split_axis=1, concat_axis=1, tiled=True)  92.1 us
    gather x2, local copies, waits for them, and re-layouts, local(): jnp.take(compact_cache, requested.reshape(-1), axis=0)  55 us
    reshape x2, local copies, waits for them, and re-layouts, local(): expert_apply(arrived, gate_proj, up_proj, down_proj)  28.2 us
    all_gather x1, blocking collectives, local(): lax.all_gather(index_weights, 'ctx', axis=0, tiled=True)  18.2 us
    unnamed x28, local copies, waits for them, and re-layouts  15.8 us
    reshape x1, local copies, waits for them, and re-layouts, local(): arrived = lax.all_to_all(copies, ('grp', 'ctx'), split_axis=1, concat_axi...  15.4 us
    all_to_all x1, starting transfers between devices, local(): lax.all_to_all(shard_terms, ('grp', 'ctx'), split_axis=1, concat_axis=1,...  14.8 us
  transfers between devices with their start and end apart: 4, of which 3 were waited for; matrix products, arithmetic and copies ran while one was open for 33% of the time, Pallas kernels for 0%

commit v1 on v0

v1 whole, which is shorter than its diff:
```python
import jax
import jax.numpy as jnp
from jax import lax
from jax.experimental import pallas as pl
from jax.experimental.pallas import tpu as pltpu
from jax.sharding import PartitionSpec as P

MESH = pl.DeviceIdType.MESH
BF16, F32 = jnp.bfloat16, jnp.float32
HEADS, LATENT, WIDTH = 128, 512, 576
IHEADS, IDIM = 64, 128
CACHE, CAP = 8192, 256
MODEL = 7168
CHUNKS = MODEL // 128
TOKW = MODEL + 128
HALF = 288
KEYB = 512
SCALE = 192.0**-0.5
ANY, VMEM, SMEM = pl.ANY, pltpu.VMEM, pltpu.SMEM


class Place:
    def __init__(self):
        self.g, self.c = lax.axis_index("grp"), lax.axis_index("ctx")
        self.z, self.core = self.g // 2, lax.rem(self.g, 2)
        self.x, self.y = self.c // 4, lax.rem(self.c, 4)

    def ctx(self, axis, d, e=0):
        dx, dy = (d, e) if axis == 0 else (e, d)
        return lax.rem(self.x + dx + 4, 4) * 4 + lax.rem(self.y + dy + 4, 4)

    def near(self, axis, d):
        return (self.g, self.ctx(axis, d))

    def peer(self, k):
        return (self.g, lax.rem(self.c + k, 16))

    def grp(self, d, other=False):
        core = 1 - self.core if other else self.core
        return lax.rem(self.z + d + 4, 4) * 2 + core

    def greet(self):
        bar = pltpu.get_barrier_semaphore()
        friends = [self.peer(k) for k in range(1, 16)]
        friends += [(self.grp(1), self.c), (self.grp(-1), self.c), (self.grp(0, True), self.c)]
        for f in friends:
            pl.semaphore_signal(bar, inc=1, device_id=f, device_id_type=MESH)
        pl.semaphore_wait(bar, len(friends))


class Post:
    def __init__(self, send_sems, recv_sems):
        self.ss, self.rs, self.out = send_sems, recv_sems, []

    def send(self, src, dst, dev):
        i = len(self.out)
        cp = pltpu.make_async_remote_copy(
            src_ref=src, dst_ref=dst, send_sem=self.ss.at[i], recv_sem=self.rs.at[i], device_id=dev, device_id_type=MESH
        )
        cp.start()
        self.out.append(cp)
        return cp

    def finish(self):
        for cp in self.out:
            cp.wait_send()


def plane_gather(post, at, part):
    def both(ref, axis):
        return post.send(ref, ref, at.near(axis, 1)), post.send(ref, ref, at.near(axis, -1))

    def split(src, h, axis, plus, minus):
        plus.wait_recv()
        lo = part(src(-1), h, 0)
        a = post.send(lo, lo, at.near(axis, 1))
        minus.wait_recv()
        hi = part(src(1), h, 1)
        return a, post.send(hi, hi, at.near(axis, -1))

    first = [both(part(at.c, h, None), h) for h in (0, 1)]
    across = {(h, 0): both(part(at.c, h, None), 1 - h) for h in (0, 1)}
    yield
    second = []
    for h in (0, 1):
        second.append(split(lambda d: at.ctx(h, d), h, h, *first[h]))
        for d in (-1, 1):
            across[h, d] = both(part(at.ctx(h, d), h, None), 1 - h)
    yield
    for h in (0, 1):
        for cp in second[h]:
            cp.wait_recv()
        across[h, 2] = both(part(at.ctx(h, 2), h, None), 1 - h)
    last = []
    for d in (0, -1, 1, 2):
        yield
        for h in (0, 1):
            last += split(lambda e: at.ctx(h, d, e), h, 1 - h, *across[h, d])
    yield
    for cp in last:
        cp.wait_recv()


def gather_kernel(
    small, pos, aq, keys, kscale,
    qall, pall, xall, scores,
    agbuf, keybuf, wb, xf, xown, lsem, ss, rs, kss, krs, zss, zrs,
):
    at = Place()
    at.greet()
    own_small = pltpu.make_async_copy(small, agbuf.at[at.c], lsem.at[0])
    own_q = pltpu.make_async_copy(aq, qall.at[at.c], lsem.at[1])
    own_pos = pltpu.make_async_copy(pos.at[at.c], pall.at[at.c], lsem.at[2])
    load_keys = pltpu.make_async_copy(keys, keybuf, lsem.at[3])
    for cp in (own_small, own_q, own_pos, load_keys):
        cp.start()
    own_small.wait()
    few = Post(kss, krs)
    quick = plane_gather(few, at, lambda i, h, q: agbuf.at[i, h] if q is None else agbuf.at[i, h, pl.ds(64 * q, 64)])
    next(quick)
    places = [few.send(pos.at[at.peer(k)[1]], pall.at[at.c], at.peer(k)) for k in range(1, 16)]
    own_q.wait()
    many = Post(ss, rs)
    big = plane_gather(
        many, at, lambda i, h, q: qall.at[i, h] if q is None else qall.at[i, h, pl.ds(HALF * q, HALF)]
    )
    next(big)
    for _ in quick:
        pass
    next(big)

    def widen(i, _):
        xf[pl.ds(pl.multiple_of(i * 128, 128), 64), :] = agbuf[i, 0, 64:128, :].astype(F32)
        xf[pl.ds(pl.multiple_of(i * 128 + 64, 64), 64), :] = agbuf[i, 1, 64:128, :].astype(F32)
        wide = [jnp.broadcast_to(xf[pl.ds(i * 128 + 64 * t + 57, 1), :], (128, 128)).T[0:64, :] for t in (0, 1)]
        wb[i] = jnp.concatenate(wide, axis=0)
        return 0

    lax.fori_loop(0, 16, widen, 0)

    def lay(k, _):
        xown[:, pl.ds(pl.multiple_of(k * 128, 128), 128)] = xf[pl.ds(k, 32, stride=64), :].astype(BF16)
        return 0

    lax.fori_loop(0, CHUNKS + 1, lay, 0)
    zpost = Post(zss, zrs)
    up, down, over = (at.grp(1), at.c), (at.grp(-1), at.c), (at.grp(0, True), at.c)
    own_x = pltpu.make_async_copy(xown, xall.at[at.g], lsem.at[4])
    own_x.start()
    z_up = zpost.send(xown, xall.at[at.g], up)
    z_down = zpost.send(xown, xall.at[at.g], down)
    z_over = [zpost.send(xown, xall.at[at.g], over)]

    load_keys.wait()

    def index_block(b, _):
        cols = pl.ds(pl.multiple_of(b * KEYB, KEYB), KEYB)
        k = keybuf[cols, :]

        def four(i, _):
            q = jnp.concatenate([agbuf[4 * i + u, t, 0:64, :] for u in range(4) for t in range(2)], axis=0)
            p = lax.dot_general(q, k, (((1,), (1,)), ((), ())), preferred_element_type=F32)
            rows = []
            for u in range(4):
                w = jnp.concatenate([wb[4 * i + u]] * (KEYB // 128), axis=1)
                a = jnp.maximum(p[u * 128 : (u + 1) * 128], 0.0) * w
                rows += [jnp.sum(a[t * 64 : (t + 1) * 64], axis=0, keepdims=True) for t in (0, 1)]
            s = jnp.concatenate(rows, axis=0) * kscale[:, cols]
            scores[pl.ds(pl.multiple_of(i * 8, 8), 8), cols] = s
            return 0

        lax.fori_loop(0, 4, four, 0)
        return 0

    blocks = CACHE // KEYB
    lax.fori_loop(0, blocks // 4, index_block, 0)
    next(big)
    lax.fori_loop(blocks // 4, blocks // 2, index_block, 0)
    next(big)
    z_up.wait_recv()
    low = xall.at[at.grp(-1)]
    z_low = zpost.send(low.at[pl.ds(0, 16)], low.at[pl.ds(0, 16)], up)
    z_over.append(zpost.send(low, low, over))
    z_down.wait_recv()
    high = xall.at[at.grp(1)]
    z_high = zpost.send(high.at[pl.ds(16, 16)], high.at[pl.ds(16, 16)], down)
    z_over.append(zpost.send(high, high, over))
    lax.fori_loop(blocks // 2, 3 * blocks // 4, index_block, 0)
    next(big)
    lax.fori_loop(3 * blocks // 4, blocks, index_block, 0)
    next(big)
    z_low.wait_recv()
    z_high.wait_recv()
    far = xall.at[at.grp(2)]
    z_over.append(zpost.send(far, far, over))
    for _ in big:
        pass
    for cp in z_over + places:
        cp.wait_recv()
    own_pos.wait()
    own_x.wait()
    for post in (few, many, zpost):
        post.finish()


def gather_all(small, pos, aq, keys, kscale):
    dma = pltpu.SemaphoreType.DMA
    return pl.pallas_call(
        gather_kernel,
        out_shape=(
            jax.ShapeDtypeStruct((16, 2, WIDTH, HEADS), BF16),
            jax.ShapeDtypeStruct((16, 8, 128), jnp.int32),
            jax.ShapeDtypeStruct((8, 32, TOKW), BF16),
            jax.ShapeDtypeStruct((32, CACHE), F32),
        ),
        in_specs=[pl.BlockSpec(memory_space=ANY)] * 4 + [pl.BlockSpec(memory_space=VMEM)],
        out_specs=(pl.BlockSpec(memory_space=ANY),) * 3 + (pl.BlockSpec(memory_space=VMEM),),
        scratch_shapes=[
            VMEM((16, 2, 128, 128), BF16),
            VMEM((CACHE, IDIM), BF16),
            VMEM((16, 128, 128), F32),
            VMEM((2048, 128), F32),
            VMEM((32, TOKW), BF16),
            dma((5,)),
            dma((40,)),
            dma((40,)),
            dma((55,)),
            dma((55,)),
            dma((8,)),
            dma((8,)),
        ],
        compiler_params=pltpu.CompilerParams(collective_id=0, has_side_effects=True, vmem_limit_bytes=48 * 2**20),
    )(small, pos, aq, keys, kscale)


def attend_kernel(pos, cache, q, o_ref, l_ref, cbuf, rows, dst, kbf, qbuf, csem, qsem):
    loads = []
    for i in range(8):
        cols = pl.ds(1024 * i, 1024)
        loads.append(pltpu.make_async_copy(cache.at[:, cols], cbuf.at[:, cols], csem.at[i]))
        loads[-1].start()
    load_q = pltpu.make_async_copy(q, qbuf, qsem)
    load_q.start()
    eye = (
        lax.broadcasted_iota(jnp.int32, (256, 256), 0) == lax.broadcasted_iota(jnp.int32, (256, 256), 1)
    ).astype(BF16)
    dst[...] = jnp.zeros_like(dst)
    for i in range(8):
        loads[i].wait()

        def turn(b, _):
            off = pl.multiple_of(i * 1024 + b * 256, 256)
            t = lax.dot_general(
                eye, cbuf[:, pl.ds(off, 256)], (((1,), (1,)), ((), ())), preferred_element_type=F32
            )
            for c in range(5):
                w = min(128, WIDTH - 128 * c)
                rows[pl.ds(off * 8 + c, 256, stride=8), 0:w] = t[:, c * 128 : c * 128 + w]
            return 0

        lax.fori_loop(0, 4, turn, 0)
    load_q.wait()

    def one(t, _):
        c, h = t // 2, lax.rem(t, 2)
        n = pos[c, 4, h]

        def pick(j, _):
            line, col = 2 * h + j // 8, lax.rem(j, 8) * 16
            for u in range(16):
                s = j * 16 + u
                p = pos[c, line, col + u]
                dst[pl.ds(pl.multiple_of(s * 8, 8), 8), :] = rows[pl.ds(pl.multiple_of(p * 8, 8), 8), :]
            return 0

        lax.fori_loop(0, (n + 15) // 16, pick, 0)
        for i in range(5):
            w = min(128, WIDTH - 128 * i)
            kbf[:, i * 128 : i * 128 + w] = dst[pl.ds(i, CAP, stride=8), 0:w].astype(BF16)
        s = jnp.dot(kbf[...], qbuf[c, h], preferred_element_type=F32) * SCALE
        live = lax.broadcasted_iota(jnp.int32, (CAP, HEADS), 0) < n
        s = jnp.where(live, s, -1e30)
        m = jnp.max(s, axis=0, keepdims=True)
        e = jnp.where(live, jnp.exp(s - m), 0.0)
        l = jnp.sum(e, axis=0, keepdims=True)
        p = (e * (1.0 / l)).T.astype(BF16)
        o_ref[c, h] = jnp.dot(p, kbf[:, 0:LATENT], preferred_element_type=F32).astype(BF16)
        l_ref[c, h] = jnp.broadcast_to(m + jnp.log(l), (8, HEADS))
        return 0

    lax.fori_loop(0, 32, one, 0)


def attend(pos, cache, q):
    return pl.pallas_call(
        attend_kernel,
        out_shape=(
            jax.ShapeDtypeStruct((16, 2, HEADS, LATENT), BF16),
            jax.ShapeDtypeStruct((16, 2, 8, HEADS), F32),
        ),
        in_specs=[pl.BlockSpec(memory_space=SMEM)] + [pl.BlockSpec(memory_space=ANY)] * 2,
        out_specs=(pl.BlockSpec(memory_space=VMEM),) * 2,
        scratch_shapes=[
            VMEM((WIDTH, CACHE), BF16),
            VMEM((CACHE * 8, 128), F32),
            VMEM((CAP * 8, 128), F32),
            VMEM((CAP, WIDTH), BF16),
            VMEM((16, 2, WIDTH, HEADS), BF16),
            pltpu.SemaphoreType.DMA((8,)),
            pltpu.SemaphoreType.DMA,
        ],
        compiler_params=pltpu.CompilerParams(vmem_limit_bytes=58 * 2**20),
    )(pos, cache, q)


def merge(parts, lo, n):
    top = parts[0][1]
    for _, l in parts[1:]:
        top = jnp.maximum(top, l)
    es = [jnp.exp(l - top) for _, l in parts]
    tot = es[0]
    for e in es[1:]:
        tot = tot + e
    inv = 1.0 / tot
    diag = lax.broadcasted_iota(jnp.int32, (n, HEADS), 0) + lo == lax.broadcasted_iota(jnp.int32, (n, HEADS), 1)
    out = None
    for (o, _), e in zip(parts, es):
        w = jnp.broadcast_to((e * inv)[0:1], (n, HEADS))
        col = jnp.sum(jnp.where(diag, w, 0.0), axis=1, keepdims=True)
        term = o.astype(F32) * col
        out = term if out is None else out + term
    return out.astype(BF16), top + jnp.log(tot)


def plane_scatter(post, at, o, l, bufs, result):
    r1, l1, m1, ml1, r2, l2, p1, pl1, r3, l3, m2, ml2, r4, l4 = bufs

    def both(src, lsrc, dst, ldst, dev):
        return post.send(src, dst, dev), post.send(lsrc, ldst, dev)

    def arrive(pair):
        for cp in pair:
            cp.wait_recv()

    s1, s2 = {}, {}
    for h in (0, 1):
        a = 1 - h
        for e in range(4):
            i = at.ctx(a, 2, e)
            s1[h, e] = both(o.at[i, h], l.at[i, h], r1.at[h, e], l1.at[h, e], at.near(a, 1 if e < 2 else -1))
    for h in (0, 1):
        a = 1 - h
        for e in range(4):
            d = 0 if e >= 2 else 1
            i = at.ctx(a, 1 - 2 * d, e)
            s2[h, d, e] = both(o.at[i, h], l.at[i, h], r2.at[h, d, e], l2.at[h, d, e], at.near(a, 1 - 2 * d))
    yield
    for e in (0, 2, 1, 3):
        for h in (0, 1):
            a = 1 - h
            d = 0 if e < 2 else 1
            i = at.ctx(a, 1 - 2 * d, e)
            arrive(s1[h, e])
            m1[h, e], ml1[h, e] = merge([(o[i, h], l[i, h]), (r1[h, e], l1[h, e])], 0, HEADS)
            s2[h, d, e] = both(m1.at[h, e], ml1.at[h, e], r2.at[h, d, e], l2.at[h, d, e], at.near(a, 1 - 2 * d))
        if e == 2:
            yield
    yield
    s3, s4 = {}, {}
    for e in (2, 1, 3, 0):
        for h in (0, 1):
            a = 1 - h
            i = at.ctx(a, 0, e)
            arrive(s2[h, 0, e])
            arrive(s2[h, 1, e])
            p1[h, e], pl1[h, e] = merge(
                [(o[i, h], l[i, h]), (r2[h, 0, e], l2[h, 0, e]), (r2[h, 1, e], l2[h, 1, e])], 0, HEADS
            )
            if e == 2:
                for d in (0, 1):
                    s3[h, d] = both(
                        p1.at[h, 2, pl.ds(64 * d, 64)], pl1.at[h, 2], r3.at[h, d], l3.at[h, d], at.near(h, 1 - 2 * d)
                    )
        yield
    for h in (0, 1):
        for d in (0, 1):
            e = 1 if d == 0 else 3
            arrive(s3[h, d])
            mine = slice(64 * d, 64 * d + 64)
            rest = slice(64 - 64 * d, 128 - 64 * d)
            m2[h, d, rest] = p1[h, e, rest]
            m2[h, d, mine], lm = merge([(p1[h, e, mine], pl1[h, e]), (r3[h, d], l3[h, d])], 64 * d, 64)
            lane = lax.broadcasted_iota(jnp.int32, (8, HEADS), 1)
            ml2[h, d] = jnp.where((lane < 64) if d == 0 else (lane >= 64), lm, pl1[h, e])
            s4[h, d] = both(m2.at[h, d], ml2.at[h, d], r4.at[h, d], l4.at[h, d], at.near(h, 1 - 2 * d))
    yield
    for h in (0, 1):
        arrive(s4[h, 0])
        arrive(s4[h, 1])
        result[h], _ = merge([(p1[h, 0], pl1[h, 0]), (r4[h, 0], l4[h, 0]), (r4[h, 1], l4[h, 1])], 0, HEADS)


def reduce_kernel(
    o, l, xall, gate, up, dn,
    attn, moe,
    xbuf, wgu, dnbuf, acc, hid, mp, rc, rz1, rz2, yf, yb, ry,
    r1, l1, m1, ml1, r2, l2, p1, pl1, r3, l3, m2, ml2, r4, l4,
    lsem, ss, rs, zss, zrs,
):
    at = Place()
    loads = [pltpu.make_async_copy(xall, xbuf, lsem.at[0])]
    for e in (0, 1):
        loads.append(pltpu.make_async_copy(gate.at[e], wgu.at[e, :, pl.ds(0, 128)], lsem.at[1 + e]))
        loads.append(pltpu.make_async_copy(up.at[e], wgu.at[e, :, pl.ds(128, 128)], lsem.at[3 + e]))
    load_dn = pltpu.make_async_copy(dn, dnbuf, lsem.at[5])
    for cp in loads + [load_dn]:
        cp.start()
    at.greet()
    post = Post(ss, rs)
    flow = plane_scatter(post, at, o, l, (r1, l1, m1, ml1, r2, l2, p1, pl1, r3, l3, m2, ml2, r4, l4), attn)
    next(flow)

    for cp in loads:
        cp.wait()
    acc[...] = jnp.zeros_like(acc)

    def expand(k, _):
        cols = pl.ds(pl.multiple_of(k * 1024, 1024), 1024)
        x = xbuf[:, :, cols].reshape(256, 1024)
        for e in (0, 1):
            acc[e] += jnp.dot(x, wgu[e, cols, :], preferred_element_type=F32)
        return 0

    lax.fori_loop(0, MODEL // 1024, expand, 0)
    gates = xbuf[:, :, MODEL:TOKW].reshape(256, 128).astype(F32)
    lane = lax.broadcasted_iota(jnp.int32, (256, 128), 1)
    for e in (0, 1):
        own = at.g * 2 + e
        col = jnp.sum(jnp.where((lane == own) | (lane == own + 16), gates, 0.0), axis=1, keepdims=True)
        gp, upart = acc[e, :, 0:128], acc[e, :, 128:256]
        hid[:, e * 128 : e * 128 + 128] = (gp / (1.0 + jnp.exp(-gp)) * upart * col).astype(BF16)
    load_dn.wait()

    def contract(k, _):
        cols = pl.ds(pl.multiple_of(k * 1024, 1024), 1024)
        mp[:, :, cols] = jnp.dot(hid[...], dnbuf[:, cols], preferred_element_type=F32).astype(BF16).reshape(8, 32, 1024)
        return 0

    lax.fori_loop(0, MODEL // 1024, contract, 0)
    zpost = Post(zss, zrs)
    zup, zdown, over = (at.grp(1), at.c), (at.grp(-1), at.c), (at.grp(0, True), at.c)
    order = (2, 1, -1, 0)
    swaps = [zpost.send(mp.at[at.grp(d, True)], rc.at[i], over) for i, d in enumerate(order)]
    next(flow)
    next(flow)

    def add(i, d):
        swaps[i].wait_recv()
        b = at.grp(d)
        mp[b] = (mp[b].astype(F32) + rc[i].astype(F32)).astype(BF16)

    add(0, 2)
    far = mp.at[at.grp(2)]
    za = zpost.send(far.at[pl.ds(0, 16)], rz1.at[0], zup)
    zb = zpost.send(far.at[pl.ds(16, 16)], rz1.at[1], zdown)
    next(flow)
    add(1, 1)
    add(2, -1)
    next(flow)
    za.wait_recv()
    b = at.grp(1)
    mp[b, 0:16] = (mp[b, 0:16].astype(F32) + rz1[0].astype(F32)).astype(BF16)
    zc = zpost.send(mp.at[b], rz2.at[0], zup)
    zb.wait_recv()
    b2 = at.grp(-1)
    mp[b2, 16:32] = (mp[b2, 16:32].astype(F32) + rz1[1].astype(F32)).astype(BF16)
    zd = zpost.send(mp.at[b2], rz2.at[1], zdown)
    swaps[3].wait_recv()
    next(flow)
    next(flow)
    zc.wait_recv()
    zd.wait_recv()

    def spread(k, _):
        cols = pl.ds(pl.multiple_of(k * 128, 128), 128)
        t = mp[at.g, :, cols].astype(F32) + rc[3, :, cols].astype(F32)
        t = t + rz2[0, :, cols].astype(F32) + rz2[1, :, cols].astype(F32)
        yf[pl.ds(k, 32, stride=CHUNKS), :] = t
        return 0

    lax.fori_loop(0, CHUNKS, spread, 0)

    def narrow(i, _):
        yb[i] = yf[pl.ds(pl.multiple_of(i * 112, 8), 112), :].astype(BF16)
        return 0

    lax.fori_loop(0, 16, narrow, 0)
    home = [zpost.send(yb.at[at.peer(k)[1]], ry.at[k - 1], at.peer(k)) for k in range(1, 16)]
    for _ in flow:
        pass
    total = yb[at.c].astype(F32)
    for k, cp in enumerate(home):
        cp.wait_recv()
        total = total + ry[k].astype(F32)
    moe[...] = total.astype(BF16)
    post.finish()
    zpost.finish()


def reduce_all(o, l, xall, gate, up, dn):
    dma = pltpu.SemaphoreType.DMA
    ob, lb = (HEADS, LATENT), (8, HEADS)

    def pair(*lead, block=ob):
        return [VMEM(lead + block, BF16), VMEM(lead + lb, F32)]

    return pl.pallas_call(
        reduce_kernel,
        out_shape=(jax.ShapeDtypeStruct((2, HEADS, LATENT), BF16), jax.ShapeDtypeStruct((112, 128), BF16)),
        in_specs=[pl.BlockSpec(memory_space=VMEM)] * 2 + [pl.BlockSpec(memory_space=ANY)] * 4,
        out_specs=(pl.BlockSpec(memory_space=VMEM),) * 2,
        scratch_shapes=[
            VMEM((8, 32, TOKW), BF16),
            VMEM((2, MODEL, 256), BF16),
            VMEM((256, MODEL), BF16),
            VMEM((2, 256, 256), F32),
            VMEM((256, 256), BF16),
            VMEM((8, 32, MODEL), BF16),
            VMEM((4, 32, MODEL), BF16),
            VMEM((2, 16, MODEL), BF16),
            VMEM((2, 32, MODEL), BF16),
            VMEM((32 * CHUNKS, 128), F32),
            VMEM((16, 112, 128), BF16),
            VMEM((15, 112, 128), BF16),
            *pair(2, 4),
            *pair(2, 4),
            *pair(2, 2, 4),
            *pair(2, 4),
            *pair(2, 2, block=(64, LATENT)),
            *pair(2, 2),
            *pair(2, 2),
            dma((6,)),
            dma((64,)),
            dma((64,)),
            dma((23,)),
            dma((23,)),
        ],
        compiler_params=pltpu.CompilerParams(collective_id=1, has_side_effects=True, vmem_limit_bytes=58 * 2**20),
    )(o, l, xall, gate, up, dn)


def local(
    index_query, index_weights, index_keys, key_scales, attn_query, compact_cache, top_pos, owner_counts,
    moe_input, expert_ids, expert_gates, gate_proj, up_proj, down_proj,
):
    experts = lax.axis_size("grp") * gate_proj.shape[0]
    matches = expert_ids[:, :, None] == jnp.arange(experts, dtype=jnp.int32)[None, None, :]
    table = jnp.sum(expert_gates[:, :, None] * matches.astype(F32), axis=1)
    high = lax.reduce_precision(table, 8, 7)
    gates = jnp.concatenate([high, table - high, jnp.zeros((2, 96), F32)], axis=1).astype(BF16)
    weights = jnp.pad(index_weights, ((0, 0), (0, 64)))
    small = jnp.concatenate(
        [
            index_query.reshape(2, IHEADS, IDIM),
            moe_input.reshape(2, CHUNKS, 128),
            gates[:, None],
            weights[:, None],
            jnp.zeros((2, 6, 128), BF16),
        ],
        axis=1,
    )
    places = jnp.transpose(top_pos, (1, 0, 2)).reshape(16, 4, 128)
    counts = jnp.pad(owner_counts.T.reshape(16, 1, 2), ((0, 0), (0, 3), (0, 126)))
    pos = jnp.concatenate([places, counts], axis=1)
    qall, pall, xall, index_scores = gather_all(
        small, pos, jnp.swapaxes(attn_query, 1, 2), index_keys, key_scales.reshape(1, CACHE)
    )
    o, l = attend(pall, compact_cache.T, qall)
    attn_out, moe_out = reduce_all(o, l, xall, gate_proj, up_proj, down_proj.reshape(256, MODEL))
    return index_scores, attn_out, moe_out.reshape(2, MODEL)


def solution(mesh):
    one = P(("grp", "ctx"))
    in_specs = (one,) * 11 + (P("grp", None, "ctx"), P("grp", None, "ctx"), P("grp", "ctx", None))
    return jax.shard_map(
        local, mesh=mesh, in_specs=in_specs, out_specs=(P("grp", "ctx"), one, one), check_vma=False
    )
```

time: 610 us -> 170 us (0.28)
  blocking collectives: 247 us -> 0 us
  Pallas kernels: 0 us -> 156 us
  local copies, waits for them, and re-layouts: 137 us -> 11.8 us
  waiting for transfers between devices: 107 us -> 0 us
  matrix products: 58.1 us -> 0 us
  starting transfers between devices: 36.9 us -> 0 us
  other arithmetic: 20.5 us -> 0.89 us
    all_gather x2 -> x0, blocking collectives: 247 us -> none  [the longest x1 229 us: local(): lax.all_gather(index_query, 'ctx', axis=0, tiled=True)]
    pallas_call x0 -> x3, Pallas kernels: none -> 156 us  [the longest x1 56.8 us: gather_all(): pl.pallas_call(gather_kernel, out_shape=(jax.ShapeDtypeStruct((16, 2, WID...]
    all_to_all x4 -> x0, waiting for transfers between devices: 107 us -> none  [the longest x1 92.1 us: local(): lax.all_to_all(served, 'ctx', split_axis=1, concat_axis=1, tiled=True)]
    dot_general x7 -> x0, matrix products: 58.1 us -> none  [the longest x1 14.7 us: local(): jnp.dot(queries.reshape(group_rows * IHEADS, IDIM), index_keys.T, preferr...]
    gather x2 -> x0, local copies, waits for them, and re-layouts: 55 us -> none  [local(): jnp.take(compact_cache, requested.reshape(-1), axis=0)]
    reshape x6 -> x3, local copies, waits for them, and re-layouts: 52.7 us -> 2.16 us  [the longest x1 1.37 us: local(): return (index_scores, attn_out, moe_out.reshape(2, MODEL))]
    all_to_all x4 -> x0, starting transfers between devices: 36.9 us -> none  [the longest x1 14.8 us: local(): lax.all_to_all(shard_terms, ('grp', 'ctx'), split_axis=1, concat_axis=1,...]
    select_n x3 -> x0, other arithmetic: 9.27 us -> none  [the longest x2 8.15 us: local(): jnp.take(compact_cache, requested.reshape(-1), axis=0)]
  transfers between devices with their start and end apart: 4 -> 0, of which waited for: 3 -> 0; matrix products, arithmetic and copies ran while one was open for 33% -> 0% of each run, Pallas kernels for 0% -> 0%
where the time goes in v1:
time: 170 us
  Pallas kernels  156 us (92%)
  local copies, waits for them, and re-layouts  11.8 us (7%)
    pallas_call x1, Pallas kernels, gather_all(): pl.pallas_call(gather_kernel, out_shape=(jax.ShapeDtypeStruct((16, 2, WID...  56.8 us
    pallas_call x1, Pallas kernels, attend(): pl.pallas_call(attend_kernel, out_shape=(jax.ShapeDtypeStruct((16, 2, HEA...  49.8 us
    pallas_call x1, Pallas kernels, reduce_all(): pl.pallas_call(reduce_kernel, out_shape=(jax.ShapeDtypeStruct((2, HEADS,...  49.5 us
    unnamed x12, local copies, waits for them, and re-layouts  8.08 us

profile of v1, /device:TPU:0, one launch (start us, length us, event | category | flops | bytes accessed | tf_op | source)
XLA Modules:
  0.0 169.6 jit_solution(15615754138260904318)
XLA Ops:
  0.6 0.7 pad_bitcast_fusion
  1.3 0.1 pad.14.clone
  1.4 0.8 select_reduce_fusion
  2.2 0.1 maximum_maximum_fusion
  2.3 0.8 copy.30
  3.0 0.8 copy.36
  3.8 0.8 copy.35
  4.6 0.1 concatenate.24.small
  4.6 0.8 copy.29
  5.5 0.0 copy-start
  5.5 1.6 copy-done
  7.1 0.0 copy-start.1
  7.1 1.0 copy-done.1
  8.0 0.0 copy-start.3
  8.0 0.8 copy-done.3
  8.8 56.8 %shard_map.157 = (bf16[16,2,576,128]{3,2,1,0:T(8,128)(2,1)}, s32[16,8,128]{2,1,0:T(8,128)S(1)}, bf16[8,32,7296]{2,1,0:T(8,128)(2,1)}, f32[32,8192]{1,0:T(8,128)S(1)}) custom-call(bf16[2,128,128]{2,1,0:T(8,128)(2,1)S(1)} %concatenate.24.small, s32[16,8,128]{2,1,0:T(8,128)S(1)} %pad_add_fusion.pos, bf16[2,576,128]{2,1,0:T(8,128)(2,1)S(1)} %bitcast.22, ...), custom_call_target="tpu_custom_call" | custom-call | tf_op jit(solution)/shard_map/pallas_call | solution.py:208
  65.6 0.0 copy-start.2
  65.6 0.6 copy-done.2
  66.2 49.8 %shard_map.158 = (bf16[16,2,128,512]{3,2,1,0:T(8,128)(2,1)}, f32[16,2,8,128]{3,2,1,0:T(8,128)}) custom-call(s32[16,8,128]{2,1,0:T(8,128)} %copy-done.2, bf16[576,8192]{1,0:T(8,128)(2,1)} %bitcast.24, bf16[16,2,576,128]{3,2,1,0:T(8,128)(2,1)} %get-tuple-element.13.q), custom_call_target="tpu_custom_call" | custom-call | tf_op jit(solution)/shard_map/pallas_call | solution.py:295
  116.0 49.5 %shard_map.159 = (bf16[2,128,512]{2,1,0:T(8,128)(2,1)}, bf16[112,128]{1,0:T(8,128)(2,1)}) custom-call(bf16[16,2,128,512]{3,2,1,0:T(8,128)(2,1)} %get-tuple-element.14.o, f32[16,2,8,128]{3,2,1,0:T(8,128)} %get-tuple-element.15.l, bf16[8,32,7296]{2,1,0:T(8,128)(2,1)} %get-tuple-element.16.xall, bf16[2,7168,128]{2,1,0:T(8,128)(2,1)} %gate.1, ...), custom_call_target="tpu_custom_call" | custom-call | tf_op jit(solution)/shard_map/pallas_call | solution.py:517
  165.6 1.4 reshape.67
  166.9 1.0 copy.39
  167.9 1.7 copy.40
  (8 shorter events, 0.1 us)
Async XLA Ops:
  5.5 1.6 copy-start
  7.1 1.0 copy-start.1
  8.0 0.8 copy-start.3
  65.6 0.6 copy-start.2

commit v2 on v1

--- a/solution.py
+++ b/solution.py
@@ -14,7 +14,8 @@
 CHUNKS = MODEL // 128
 TOKW = MODEL + 128
 HALF = 288
-KEYB = 512
+KEYB = 2048
+PITCH = 5
 SCALE = 192.0**-0.5
 ANY, VMEM, SMEM = pl.ANY, pltpu.VMEM, pltpu.SMEM
 
@@ -102,44 +103,99 @@
 
 
 def gather_kernel(
-    small, pos, aq, keys, kscale,
-    qall, pall, xall, scores,
-    agbuf, keybuf, wb, xf, xown, lsem, ss, rs, kss, krs, zss, zrs,
+    iq, iw, tok, ids, eg, tp, oc, kscale, aq, keys, cache,
+    qall, pall, xall, kg, scores,
+    stage, pst, agbuf, keybuf, xa, xown, qbuf, wt, cbuf, rows, dst, kbf, posv, poss,
+    csem, ksem, lsem, ss, rs, kss, krs, zss, zrs,
 ):
     at = Place()
+    loads = []
+    for i in range(8):
+        cols = pl.ds(1024 * i, 1024)
+        loads.append(pltpu.make_async_copy(cache.at[:, cols], cbuf.at[:, cols], csem.at[i]))
+        loads[-1].start()
+    own_q = pltpu.make_async_copy(aq, qall.at[at.c], lsem.at[1])
+    own_q.start()
+    load_keys = pltpu.make_async_copy(keys, keybuf, lsem.at[3])
+    load_keys.start()
+
+    stage[...] = jnp.zeros_like(stage)
+    for j in range(IHEADS):
+        stage[pl.ds(j, 2, stride=128), :] = iq[:, 128 * j : 128 * j + 128].astype(F32)
+    for k in range(CHUNKS):
+        stage[pl.ds(64 + k, 2, stride=128), :] = tok[:, 128 * k : 128 * k + 128].astype(F32)
+    lane = lax.broadcasted_iota(jnp.int32, (2, 128), 1)
+    table = jnp.zeros((2, 128), F32)
+    for k in range(8):
+        mine = (lane == ids[:, k : k + 1]) | (lane == ids[:, k : k + 1] + 16)
+        table = table + jnp.where(mine, eg[:, k : k + 1], 0.0)
+    high = table.astype(BF16).astype(F32)
+    stage[pl.ds(120, 2, stride=128), :] = jnp.where(lane < 16, high, table - high)
+    stage[pl.ds(121, 2, stride=128), 0:IHEADS] = iw[...].astype(F32)
+    agbuf[at.c] = stage[...].reshape(2, 128, 128).astype(BF16)
+    first_lane = lax.broadcasted_iota(jnp.int32, (1, 128), 1)
+    for o in range(16):
+        for h in (0, 1):
+            for k in (0, 1):
+                pst[o, 2 * h + k : 2 * h + k + 1, :] = tp[h, o : o + 1, 128 * k : 128 * k + 128] * PITCH
+        pst[o, 4:5, :] = jnp.where(first_lane == 0, oc[0:1, o : o + 1], oc[1:2, o : o + 1])
+        pst[o, 5:8, :] = jnp.zeros((3, 128), jnp.int32)
     at.greet()
-    own_small = pltpu.make_async_copy(small, agbuf.at[at.c], lsem.at[0])
-    own_q = pltpu.make_async_copy(aq, qall.at[at.c], lsem.at[1])
-    own_pos = pltpu.make_async_copy(pos.at[at.c], pall.at[at.c], lsem.at[2])
-    load_keys = pltpu.make_async_copy(keys, keybuf, lsem.at[3])
-    for cp in (own_small, own_q, own_pos, load_keys):
-        cp.start()
-    own_small.wait()
     few = Post(kss, krs)
     quick = plane_gather(few, at, lambda i, h, q: agbuf.at[i, h] if q is None else agbuf.at[i, h, pl.ds(64 * q, 64)])
     next(quick)
-    places = [few.send(pos.at[at.peer(k)[1]], pall.at[at.c], at.peer(k)) for k in range(1, 16)]
+    places = [few.send(pst.at[at.peer(k)[1]], posv.at[at.c], at.peer(k)) for k in range(1, 16)]
+    own_pos = pltpu.make_async_copy(pst.at[at.c], posv.at[at.c], lsem.at[2])
+    own_pos.start()
     own_q.wait()
     many = Post(ss, rs)
     big = plane_gather(
         many, at, lambda i, h, q: qall.at[i, h] if q is None else qall.at[i, h, pl.ds(HALF * q, HALF)]
     )
     next(big)
+
+    eye = (
+        lax.broadcasted_iota(jnp.int32, (256, 256), 0) == lax.broadcasted_iota(jnp.int32, (256, 256), 1)
+    ).astype(BF16)
+
+    def turn_rows(i):
+        loads[i].wait()
+
+        def turn(b, _):
+            off = pl.multiple_of(i * 1024 + b * 256, 256)
+            t = lax.dot_general(
+                eye, cbuf[:, pl.ds(off, 256)], (((1,), (1,)), ((), ())), preferred_element_type=F32
+            )
+            for c in range(5):
+                w = min(128, WIDTH - 128 * c)
+                rows[pl.ds(off * PITCH + c, 256, stride=PITCH), 0:w] = t[:, c * 128 : c * 128 + w]
+            return 0
+
+        lax.fori_loop(0, 4, turn, 0)
+
+    turn_rows(0)
+    next(quick)
+    turn_rows(1)
+    next(quick)
+    turn_rows(2)
+    next(quick)
+    next(quick)
+    next(quick)
+    turn_rows(3)
+    next(quick)
+    next(big)
+    turn_rows(4)
     for _ in quick:
         pass
-    next(big)
 
     def widen(i, _):
-        xf[pl.ds(pl.multiple_of(i * 128, 128), 64), :] = agbuf[i, 0, 64:128, :].astype(F32)
-        xf[pl.ds(pl.multiple_of(i * 128 + 64, 64), 64), :] = agbuf[i, 1, 64:128, :].astype(F32)
-        wide = [jnp.broadcast_to(xf[pl.ds(i * 128 + 64 * t + 57, 1), :], (128, 128)).T[0:64, :] for t in (0, 1)]
-        wb[i] = jnp.concatenate(wide, axis=0)
+        xa[pl.ds(pl.multiple_of(i * 256, 256), 256), :] = agbuf[i].reshape(256, 128).astype(F32)
         return 0
 
     lax.fori_loop(0, 16, widen, 0)
 
     def lay(k, _):
-        xown[:, pl.ds(pl.multiple_of(k * 128, 128), 128)] = xf[pl.ds(k, 32, stride=64), :].astype(BF16)
+        xown[:, pl.ds(pl.multiple_of(k * 128, 128), 128)] = xa[pl.ds(64 + k, 32, stride=128), :].astype(BF16)
         return 0
 
     lax.fori_loop(0, CHUNKS + 1, lay, 0)
@@ -150,60 +206,109 @@
     z_up = zpost.send(xown, xall.at[at.g], up)
     z_down = zpost.send(xown, xall.at[at.g], down)
     z_over = [zpost.send(xown, xall.at[at.g], over)]
-
+    for cp in places:
+        cp.wait_recv()
+    own_pos.wait()
+    to_smem = pltpu.make_async_copy(posv, poss, lsem.at[0])
+    to_smem.start()
+    keep_pos = pltpu.make_async_copy(posv, pall, lsem.at[2])
+    keep_pos.start()
+
+    def lay_q(j, _):
+        qbuf[pl.ds(pl.multiple_of(j * 32, 32), 32), :] = xa[pl.ds(j, 32, stride=128), :].astype(BF16)
+        return 0
+
+    lax.fori_loop(0, IHEADS, lay_q, 0)
+    wt[...] = jnp.concatenate([xa[pl.ds(121, 32, stride=128), :], jnp.zeros((96, 128), F32)], axis=0).T
+    w = jnp.concatenate([wt[pl.ds(u, 16, stride=4), 0:32] for u in range(4)], axis=1)
+    turn_rows(5)
+    turn_rows(6)
+    turn_rows(7)
+    next(big)
     load_keys.wait()
 
     def index_block(b, _):
-        cols = pl.ds(pl.multiple_of(b * KEYB, KEYB), KEYB)
-        k = keybuf[cols, :]
-
-        def four(i, _):
-            q = jnp.concatenate([agbuf[4 * i + u, t, 0:64, :] for u in range(4) for t in range(2)], axis=0)
-            p = lax.dot_general(q, k, (((1,), (1,)), ((), ())), preferred_element_type=F32)
-            rows = []
-            for u in range(4):
-                w = jnp.concatenate([wb[4 * i + u]] * (KEYB // 128), axis=1)
-                a = jnp.maximum(p[u * 128 : (u + 1) * 128], 0.0) * w
-                rows += [jnp.sum(a[t * 64 : (t + 1) * 64], axis=0, keepdims=True) for t in (0, 1)]
-            s = jnp.concatenate(rows, axis=0) * kscale[:, cols]
-            scores[pl.ds(pl.multiple_of(i * 8, 8), 8), cols] = s
-            return 0
-
-        lax.fori_loop(0, 4, four, 0)
-        return 0
-
-    blocks = CACHE // KEYB
-    lax.fori_loop(0, blocks // 4, index_block, 0)
+        k = keybuf[pl.ds(pl.multiple_of(b * KEYB, KEYB), KEYB), :]
+        a = None
+        for i in range(8):
+            p = lax.dot_general(
+                k, qbuf[i * 256 : i * 256 + 256, :], (((1,), (1,)), ((), ())), preferred_element_type=F32
+            )
+            for u in (0, 1):
+                t = jnp.maximum(p[:, u * 128 : u * 128 + 128], 0.0) * w[2 * i + u : 2 * i + u + 1, :]
+                a = t if a is None else a + t
+        a = a + pltpu.roll(a, 64, 1)
+        a = (a + pltpu.roll(a, 32, 1)).T
+        n = KEYB // 128
+        scale = kscale[pl.ds(pl.multiple_of(b * n, n), n), :]
+        for j in range(n):
+            cols = pl.ds(pl.multiple_of(b * KEYB + j * 128, 128), 128)
+            scores[:, cols] = a[0:32, j * 128 : j * 128 + 128] * scale[j : j + 1, :]
+        return 0
+
+    def index(b):
+        lax.fori_loop(b, b + 1, index_block, 0)
+
+    index(0)
     next(big)
-    lax.fori_loop(blocks // 4, blocks // 2, index_block, 0)
+    index(1)
     next(big)
     z_up.wait_recv()
     low = xall.at[at.grp(-1)]
     z_low = zpost.send(low.at[pl.ds(0, 16)], low.at[pl.ds(0, 16)], up)
     z_over.append(zpost.send(low, low, over))
     z_down.wait_recv()
-    high = xall.at[at.grp(1)]
-    z_high = zpost.send(high.at[pl.ds(16, 16)], high.at[pl.ds(16, 16)], down)
-    z_over.append(zpost.send(high, high, over))
-    lax.fori_loop(blocks // 2, 3 * blocks // 4, index_block, 0)
+    high_x = xall.at[at.grp(1)]
+    z_high = zpost.send(high_x.at[pl.ds(16, 16)], high_x.at[pl.ds(16, 16)], down)
+    z_over.append(zpost.send(high_x, high_x, over))
+    index(2)
     next(big)
-    lax.fori_loop(3 * blocks // 4, blocks, index_block, 0)
+    index(3)
     next(big)
+    to_smem.wait()
+
+    def select(t, _):
+        c, line = t // 2, lax.rem(t, 2) * 2
+
+        def pick(j, _):
+            for u in range(64):
+                p = poss[c, line + j // 2, lax.rem(j, 2) * 64 + u]
+                dst[pl.ds((j * 64 + u) * PITCH, 8), :] = rows[pl.ds(p, 8), :]
+            return 0
+
+        lax.fori_loop(0, CAP // 64, pick, 0)
+        for i in range(5):
+            n = min(128, WIDTH - 128 * i)
+            kbf[t, :, i * 128 : i * 128 + n] = dst[pl.ds(i, CAP, stride=PITCH), 0:n].astype(BF16)
+        return 0
+
+    keeps = []
+
+    def select_rows(i):
+        lax.fori_loop(8 * i, 8 * i + 8, select, 0)
+        part = pl.ds(8 * i, 8)
+        keeps.append(pltpu.make_async_copy(kbf.at[part], kg.at[part], ksem.at[i]))
+        keeps[-1].start()
+
+    select_rows(0)
     z_low.wait_recv()
     z_high.wait_recv()
     far = xall.at[at.grp(2)]
     z_over.append(zpost.send(far, far, over))
+    select_rows(1)
+    select_rows(2)
+    select_rows(3)
     for _ in big:
         pass
-    for cp in z_over + places:
+    for cp in z_over:
         cp.wait_recv()
-    own_pos.wait()
-    own_x.wait()
+    for cp in keeps + [own_x, keep_pos]:
+        cp.wait()
     for post in (few, many, zpost):
         post.finish()
 
 
-def gather_all(small, pos, aq, keys, kscale):
+def gather_all(*args):
     dma = pltpu.SemaphoreType.DMA
     return pl.pallas_call(
         gather_kernel,
@@ -211,16 +316,28 @@
             jax.ShapeDtypeStruct((16, 2, WIDTH, HEADS), BF16),
             jax.ShapeDtypeStruct((16, 8, 128), jnp.int32),
             jax.ShapeDtypeStruct((8, 32, TOKW), BF16),
+            jax.ShapeDtypeStruct((32, CAP, WIDTH), BF16),
             jax.ShapeDtypeStruct((32, CACHE), F32),
         ),
-        in_specs=[pl.BlockSpec(memory_space=ANY)] * 4 + [pl.BlockSpec(memory_space=VMEM)],
-        out_specs=(pl.BlockSpec(memory_space=ANY),) * 3 + (pl.BlockSpec(memory_space=VMEM),),
+        in_specs=[pl.BlockSpec(memory_space=VMEM)] * 8 + [pl.BlockSpec(memory_space=ANY)] * 3,
+        out_specs=(pl.BlockSpec(memory_space=ANY),) * 4 + (pl.BlockSpec(memory_space=VMEM),),
         scratch_shapes=[
+            VMEM((256, 128), F32),
+            VMEM((16, 8, 128), jnp.int32),
             VMEM((16, 2, 128, 128), BF16),
             VMEM((CACHE, IDIM), BF16),
-            VMEM((16, 128, 128), F32),
-            VMEM((2048, 128), F32),
+            VMEM((32 * 128, 128), F32),
             VMEM((32, TOKW), BF16),
+            VMEM((IHEADS * 32, 128), BF16),
+            VMEM((128, 128), F32),
+            VMEM((WIDTH, CACHE), BF16),
+            VMEM((CACHE * PITCH + 8, 128), F32),
+            VMEM((CAP * PITCH + 8, 128), F32),
+            VMEM((32, CAP, WIDTH), BF16),
+            VMEM((16, 8, 128), jnp.int32),
+            SMEM((16, 8, 128), jnp.int32),
+            dma((8,)),
+            dma((4,)),
             dma((5,)),
             dma((40,)),
             dma((40,)),
@@ -229,88 +346,8 @@
             dma((8,)),
             dma((8,)),
         ],
-        compiler_params=pltpu.CompilerParams(collective_id=0, has_side_effects=True, vmem_limit_bytes=48 * 2**20),
-    )(small, pos, aq, keys, kscale)
-
-
-def attend_kernel(pos, cache, q, o_ref, l_ref, cbuf, rows, dst, kbf, qbuf, csem, qsem):
-    loads = []
-    for i in range(8):
-        cols = pl.ds(1024 * i, 1024)
-        loads.append(pltpu.make_async_copy(cache.at[:, cols], cbuf.at[:, cols], csem.at[i]))
-        loads[-1].start()
-    load_q = pltpu.make_async_copy(q, qbuf, qsem)
-    load_q.start()
-    eye = (
-        lax.broadcasted_iota(jnp.int32, (256, 256), 0) == lax.broadcasted_iota(jnp.int32, (256, 256), 1)
-    ).astype(BF16)
-    dst[...] = jnp.zeros_like(dst)
-    for i in range(8):
-        loads[i].wait()
-
-        def turn(b, _):
-            off = pl.multiple_of(i * 1024 + b * 256, 256)
-            t = lax.dot_general(
-                eye, cbuf[:, pl.ds(off, 256)], (((1,), (1,)), ((), ())), preferred_element_type=F32
-            )
-            for c in range(5):
-                w = min(128, WIDTH - 128 * c)
-                rows[pl.ds(off * 8 + c, 256, stride=8), 0:w] = t[:, c * 128 : c * 128 + w]
-            return 0
-
-        lax.fori_loop(0, 4, turn, 0)
-    load_q.wait()
-
-    def one(t, _):
-        c, h = t // 2, lax.rem(t, 2)
-        n = pos[c, 4, h]
-
-        def pick(j, _):
-            line, col = 2 * h + j // 8, lax.rem(j, 8) * 16
-            for u in range(16):
-                s = j * 16 + u
-                p = pos[c, line, col + u]
-                dst[pl.ds(pl.multiple_of(s * 8, 8), 8), :] = rows[pl.ds(pl.multiple_of(p * 8, 8), 8), :]
-            return 0
-
-        lax.fori_loop(0, (n + 15) // 16, pick, 0)
-        for i in range(5):
-            w = min(128, WIDTH - 128 * i)
-            kbf[:, i * 128 : i * 128 + w] = dst[pl.ds(i, CAP, stride=8), 0:w].astype(BF16)
-        s = jnp.dot(kbf[...], qbuf[c, h], preferred_element_type=F32) * SCALE
-        live = lax.broadcasted_iota(jnp.int32, (CAP, HEADS), 0) < n
-        s = jnp.where(live, s, -1e30)
-        m = jnp.max(s, axis=0, keepdims=True)
-        e = jnp.where(live, jnp.exp(s - m), 0.0)
-        l = jnp.sum(e, axis=0, keepdims=True)
-        p = (e * (1.0 / l)).T.astype(BF16)
-        o_ref[c, h] = jnp.dot(p, kbf[:, 0:LATENT], preferred_element_type=F32).astype(BF16)
-        l_ref[c, h] = jnp.broadcast_to(m + jnp.log(l), (8, HEADS))
-        return 0
-
-    lax.fori_loop(0, 32, one, 0)
-
-
-def attend(pos, cache, q):
-    return pl.pallas_call(
-        attend_kernel,
-        out_shape=(
-            jax.ShapeDtypeStruct((16, 2, HEADS, LATENT), BF16),
-            jax.ShapeDtypeStruct((16, 2, 8, HEADS), F32),
-        ),
-        in_specs=[pl.BlockSpec(memory_space=SMEM)] + [pl.BlockSpec(memory_space=ANY)] * 2,
-        out_specs=(pl.BlockSpec(memory_space=VMEM),) * 2,
-        scratch_shapes=[
-            VMEM((WIDTH, CACHE), BF16),
-            VMEM((CACHE * 8, 128), F32),
-            VMEM((CAP * 8, 128), F32),
-            VMEM((CAP, WIDTH), BF16),
-            VMEM((16, 2, WIDTH, HEADS), BF16),
-            pltpu.SemaphoreType.DMA((8,)),
-            pltpu.SemaphoreType.DMA,
-        ],
-        compiler_params=pltpu.CompilerParams(vmem_limit_bytes=58 * 2**20),
-    )(pos, cache, q)
+        compiler_params=pltpu.CompilerParams(collective_id=0, has_side_effects=True, vmem_limit_bytes=58 * 2**20),
+    )(*args)
 
 
 def merge(parts, lo, n):
@@ -332,7 +369,24 @@
     return out.astype(BF16), top + jnp.log(tot)
 
 
-def plane_scatter(post, at, o, l, bufs, result):
+def attend_rows(at, counts, kbuf, qbuf, o, l, h, d):
+    ids = [at.ctx(1 - h, d, e) for e in range(4)]
+    ss = [jnp.dot(kbuf[2 * i + h], qbuf[i, h], preferred_element_type=F32) * SCALE for i in ids]
+    ps = []
+    for i, s in zip(ids, ss):
+        live = lax.broadcasted_iota(jnp.int32, (CAP, HEADS), 0) < counts[i, 4, h]
+        s = jnp.where(live, s, -1e30)
+        m = jnp.max(s, axis=0, keepdims=True)
+        e = jnp.where(live, jnp.exp(s - m), 0.0)
+        n = jnp.sum(e, axis=0, keepdims=True)
+        l[i, h] = jnp.broadcast_to(m + jnp.log(n), (8, HEADS))
+        ps.append((e * (1.0 / n)).astype(BF16))
+    for i, p in zip(ids, ps):
+        v = kbuf[2 * i + h, :, 0:LATENT]
+        o[i, h] = lax.dot_general(p, v, (((0,), (0,)), ((), ())), preferred_element_type=F32).astype(BF16)
+
+
+def plane_scatter(post, at, work, o, l, bufs, result):
     r1, l1, m1, ml1, r2, l2, p1, pl1, r3, l3, m2, ml2, r4, l4 = bufs
 
     def both(src, lsrc, dst, ldst, dev):
@@ -345,11 +399,15 @@
     s1, s2 = {}, {}
     for h in (0, 1):
         a = 1 - h
+        work(h, 2)
         for e in range(4):
             i = at.ctx(a, 2, e)
             s1[h, e] = both(o.at[i, h], l.at[i, h], r1.at[h, e], l1.at[h, e], at.near(a, 1 if e < 2 else -1))
+    yield
     for h in (0, 1):
         a = 1 - h
+        work(h, 1)
+        work(h, -1)
         for e in range(4):
             d = 0 if e >= 2 else 1
             i = at.ctx(a, 1 - 2 * d, e)
@@ -365,6 +423,8 @@
             s2[h, d, e] = both(m1.at[h, e], ml1.at[h, e], r2.at[h, d, e], l2.at[h, d, e], at.near(a, 1 - 2 * d))
         if e == 2:
             yield
+    work(0, 0)
+    work(1, 0)
     yield
     s3, s4 = {}, {}
     for e in (2, 1, 3, 0):
@@ -401,13 +461,34 @@
 
 
 def reduce_kernel(
-    o, l, xall, gate, up, dn,
+    counts, kg, qall, xall, gate, up, dn,
     attn, moe,
+    kbuf, qbuf, o, l, tot,
     xbuf, wgu, dnbuf, acc, hid, mp, rc, rz1, rz2, yf, yb, ry,
     r1, l1, m1, ml1, r2, l2, p1, pl1, r3, l3, m2, ml2, r4, l4,
-    lsem, ss, rs, zss, zrs,
+    rsem, lsem, ss, rs, zss, zrs,
 ):
     at = Place()
+    near = {}
+    for dx, dy in [(2, 2), (0, 2), (1, 2), (3, 2), (2, 0), (2, 1), (2, 3)] + [
+        (dx, dy) for dx in (0, 1, 3) for dy in (0, 1, 3)
+    ]:
+        i = at.ctx(0, dx, dy)
+        n = len(near)
+        pair = pl.ds(2 * i, 2)
+        near[dx, dy] = [
+            pltpu.make_async_copy(kg.at[pair], kbuf.at[pair], rsem.at[2 * n]),
+            pltpu.make_async_copy(qall.at[i], qbuf.at[i], rsem.at[2 * n + 1]),
+        ]
+        for cp in near[dx, dy]:
+            cp.start()
+
+    def work(h, d):
+        for e in range(4):
+            for cp in near.pop((e, d % 4) if h == 0 else (d % 4, e), ()):
+                cp.wait()
+        attend_rows(at, counts, kbuf, qbuf, o, l, h, d)
+
     loads = [pltpu.make_async_copy(xall, xbuf, lsem.at[0])]
     for e in (0, 1):
         loads.append(pltpu.make_async_copy(gate.at[e], wgu.at[e, :, pl.ds(0, 128)], lsem.at[1 + e]))
@@ -417,7 +498,7 @@
         cp.start()
     at.greet()
     post = Post(ss, rs)
-    flow = plane_scatter(post, at, o, l, (r1, l1, m1, ml1, r2, l2, p1, pl1, r3, l3, m2, ml2, r4, l4), attn)
+    flow = plane_scatter(post, at, work, o, l, (r1, l1, m1, ml1, r2, l2, p1, pl1, r3, l3, m2, ml2, r4, l4), attn)
     next(flow)
 
     for cp in loads:
@@ -432,6 +513,7 @@
         return 0
 
     lax.fori_loop(0, MODEL // 1024, expand, 0)
+    next(flow)
     gates = xbuf[:, :, MODEL:TOKW].reshape(256, 128).astype(F32)
     lane = lax.broadcasted_iota(jnp.int32, (256, 128), 1)
     for e in (0, 1):
@@ -502,12 +584,14 @@
     for k, cp in enumerate(home):
         cp.wait_recv()
         total = total + ry[k].astype(F32)
-    moe[...] = total.astype(BF16)
+    tot[...] = total
+    for k in range(CHUNKS):
+        moe[:, 128 * k : 128 * k + 128] = tot[pl.ds(k, 2, stride=CHUNKS), :].astype(BF16)
     post.finish()
     zpost.finish()
 
 
-def reduce_all(o, l, xall, gate, up, dn):
+def reduce_all(*args):
     dma = pltpu.SemaphoreType.DMA
     ob, lb = (HEADS, LATENT), (8, HEADS)
 
@@ -516,10 +600,15 @@
 
     return pl.pallas_call(
         reduce_kernel,
-        out_shape=(jax.ShapeDtypeStruct((2, HEADS, LATENT), BF16), jax.ShapeDtypeStruct((112, 128), BF16)),
-        in_specs=[pl.BlockSpec(memory_space=VMEM)] * 2 + [pl.BlockSpec(memory_space=ANY)] * 4,
+        out_shape=(jax.ShapeDtypeStruct((2, HEADS, LATENT), BF16), jax.ShapeDtypeStruct((2, MODEL), BF16)),
+        in_specs=[pl.BlockSpec(memory_space=SMEM)] + [pl.BlockSpec(memory_space=ANY)] * 6,
         out_specs=(pl.BlockSpec(memory_space=VMEM),) * 2,
         scratch_shapes=[
+            VMEM((32, CAP, WIDTH), BF16),
+            VMEM((16, 2, WIDTH, HEADS), BF16),
+            VMEM((16, 2) + ob, BF16),
+            VMEM((16, 2) + lb, F32),
+            VMEM((112, 128), F32),
             VMEM((8, 32, TOKW), BF16),
             VMEM((2, MODEL, 256), BF16),
             VMEM((256, MODEL), BF16),
@@ -539,6 +628,7 @@
             *pair(2, 2, block=(64, LATENT)),
             *pair(2, 2),
             *pair(2, 2),
+            dma((32,)),
             dma((6,)),
             dma((64,)),
             dma((64,)),
@@ -546,38 +636,21 @@
             dma((23,)),
         ],
         compiler_params=pltpu.CompilerParams(collective_id=1, has_side_effects=True, vmem_limit_bytes=58 * 2**20),
-    )(o, l, xall, gate, up, dn)
+    )(*args)
 
 
 def local(
     index_query, index_weights, index_keys, key_scales, attn_query, compact_cache, top_pos, owner_counts,
     moe_input, expert_ids, expert_gates, gate_proj, up_proj, down_proj,
 ):
-    experts = lax.axis_size("grp") * gate_proj.shape[0]
-    matches = expert_ids[:, :, None] == jnp.arange(experts, dtype=jnp.int32)[None, None, :]
-    table = jnp.sum(expert_gates[:, :, None] * matches.astype(F32), axis=1)
-    high = lax.reduce_precision(table, 8, 7)
-    gates = jnp.concatenate([high, table - high, jnp.zeros((2, 96), F32)], axis=1).astype(BF16)
-    weights = jnp.pad(index_weights, ((0, 0), (0, 64)))
-    small = jnp.concatenate(
-        [
-            index_query.reshape(2, IHEADS, IDIM),
-            moe_input.reshape(2, CHUNKS, 128),
-            gates[:, None],
-            weights[:, None],
-            jnp.zeros((2, 6, 128), BF16),
-        ],
-        axis=1,
+    qall, pall, xall, kg, index_scores = gather_all(
+        index_query, index_weights, moe_input, expert_ids, expert_gates, top_pos, owner_counts,
+        key_scales.reshape(CACHE // 128, 128), jnp.swapaxes(attn_query, 1, 2), index_keys, compact_cache.T,
     )
-    places = jnp.transpose(top_pos, (1, 0, 2)).reshape(16, 4, 128)
-    counts = jnp.pad(owner_counts.T.reshape(16, 1, 2), ((0, 0), (0, 3), (0, 126)))
-    pos = jnp.concatenate([places, counts], axis=1)
-    qall, pall, xall, index_scores = gather_all(
-        small, pos, jnp.swapaxes(attn_query, 1, 2), index_keys, key_scales.reshape(1, CACHE)
+    attn_out, moe_out = reduce_all(
+        pall, kg, qall, xall, gate_proj, up_proj, down_proj.reshape(256, MODEL)
     )
-    o, l = attend(pall, compact_cache.T, qall)
-    attn_out, moe_out = reduce_all(o, l, xall, gate_proj, up_proj, down_proj.reshape(256, MODEL))
-    return index_scores, attn_out, moe_out.reshape(2, MODEL)
+    return index_scores, attn_out, moe_out
 
 
 def solution(mesh):

time: 170 us -> 136 us (0.80)
  Pallas kernels: 156 us -> 131 us
  local copies, waits for them, and re-layouts: 11.8 us -> 4.02 us
    pallas_call x1 -> x0, Pallas kernels: 49.8 us -> none  [attend(): pl.pallas_call(attend_kernel, out_shape=(jax.ShapeDtypeStruct((16, 2, HEA...]
    pallas_call x1, Pallas kernels: 56.8 us -> 79 us  [gather_all(): pl.pallas_call(gather_kernel, out_shape=(jax.ShapeDtypeStruct((16, 2, WID...]
    unnamed x12 -> x5, local copies, waits for them, and re-layouts: 8.08 us -> 4.02 us
    pallas_call x1, Pallas kernels: 49.5 us -> 52.2 us  [reduce_all(): pl.pallas_call(reduce_kernel, out_shape=(jax.ShapeDtypeStruct((2, HEADS,...]
    reshape x3 -> x0, local copies, waits for them, and re-layouts: 2.16 us -> none  [the longest x1 1.37 us: local(): return (index_scores, attn_out, moe_out.reshape(2, MODEL))]
where the time goes in v2:
time: 136 us
  Pallas kernels  131 us (96%)
  local copies, waits for them, and re-layouts  4.02 us (3%)
    pallas_call x1, Pallas kernels, gather_all(): pl.pallas_call(gather_kernel, out_shape=(jax.ShapeDtypeStruct((16, 2, WID...  79 us
    pallas_call x1, Pallas kernels, reduce_all(): pl.pallas_call(reduce_kernel, out_shape=(jax.ShapeDtypeStruct((2, HEADS,...  52.2 us
    unnamed x5, local copies, waits for them, and re-layouts  4.02 us

profile of v2, /device:TPU:0, one launch (start us, length us, event | category | flops | bytes accessed | tf_op | source)
XLA Modules:
  0.0 135.8 jit_solution(3740798729290752509)
XLA Ops:
  0.6 79.0 %shard_map.157 = (bf16[16,2,576,128]{3,2,1,0:T(8,128)(2,1)}, s32[16,8,128]{2,1,0:T(8,128)}, bf16[8,32,7296]{2,1,0:T(8,128)(2,1)}, bf16[32,256,576]{2,1,0:T(8,128)(2,1)}, f32[32,8192]{1,0:T(8,128)}) custom-call(bf16[2,8192]{1,0:T(2,128)(2,1)} %iq.1, bf16[2,64]{1,0:T(2,128)(2,1)} %iw.1, bf16[2,7168]{1,0:T(2,128)(2,1)} %tok.1, s32[2,8]{1,0:T(2,128)} %ids.1, ...), custom_call_target="tpu_custom_call" | custom-call | tf_op jit(solution)/shard_map/pallas_call | solution.py:313
  79.6 0.0 copy-start
  79.6 52.2 %shard_map.158 = (bf16[2,128,512]{2,1,0:T(8,128)(2,1)}, bf16[2,7168]{1,0:T(2,128)(2,1)}) custom-call(s32[16,8,128]{2,1,0:T(8,128)} %get-tuple-element.11.counts, bf16[32,256,576]{2,1,0:T(8,128)(2,1)} %get-tuple-element.12.kg, bf16[16,2,576,128]{3,2,1,0:T(8,128)(2,1)} %get-tuple-element.13.qall, bf16[8,32,7296]{2,1,0:T(8,128)(2,1)} %get-tuple-element.14.xall, ...), custom_call_target="tpu_custom_call" | custom-call | tf_op jit(solution)/shard_map/pallas_call | solution.py:601
  131.8 0.0 copy-done
  131.8 1.0 copy.20
  132.8 1.7 %copy.21 = bf16[2,128,512]{2,1,0:T(8,128)(2,1)} copy(bf16[2,128,512]{2,1,0:T(8,128)(2,1)} %get-tuple-element.21) | data formatting | bytes 524288
  134.5 1.4 %copy.22 = bf16[2,7168]{1,0:T(2,128)(2,1)} copy(bf16[2,7168]{1,0:T(2,128)(2,1)} %get-tuple-element.22) | data formatting | bytes 57344
Async XLA Ops:
  79.6 52.2 %copy-start = (f32[32,8192]{1,0:T(8,128)S(1)}, f32[32,8192]{1,0:T(8,128)}, u32[]{:S(2)}) copy-start(f32[32,8192]{1,0:T(8,128)} %get-tuple-element.20) | copy-start | bytes 3145732

commit v3 on v2

--- a/solution.py
+++ b/solution.py
@@ -105,7 +105,7 @@
 def gather_kernel(
     iq, iw, tok, ids, eg, tp, oc, kscale, aq, keys, cache,
     qall, pall, xall, kg, scores,
-    stage, pst, agbuf, keybuf, xa, xown, qbuf, wt, cbuf, rows, dst, kbf, posv, poss,
+    stage, pst, agbuf, keybuf, xa, xown, qbuf, wt, wq, cbuf, rows, dst, kbf, posv, poss,
     csem, ksem, lsem, ss, rs, kss, krs, zss, zrs,
 ):
     at = Place()
@@ -161,32 +161,59 @@
     def turn_rows(i):
         loads[i].wait()
 
-        def turn(b, _):
-            off = pl.multiple_of(i * 1024 + b * 256, 256)
-            t = lax.dot_general(
-                eye, cbuf[:, pl.ds(off, 256)], (((1,), (1,)), ((), ())), preferred_element_type=F32
-            )
+        for b in range(4):
+            off = i * 1024 + b * 256
+            x = cbuf[:, off : off + 256]
+            if b < 3:
+                t = x.T.astype(F32)
+            else:
+                t = lax.dot_general(eye, x, (((1,), (1,)), ((), ())), preferred_element_type=F32)
             for c in range(5):
                 w = min(128, WIDTH - 128 * c)
                 rows[pl.ds(off * PITCH + c, 256, stride=PITCH), 0:w] = t[:, c * 128 : c * 128 + w]
-            return 0
-
-        lax.fori_loop(0, 4, turn, 0)
-
-    turn_rows(0)
+
+    def select(t, _):
+        c, line = t // 2, lax.rem(t, 2) * 2
+        for u in range(CAP):
+            p = poss[c, line + u // 128, u % 128]
+            dst[pl.ds(u * PITCH, 8), :] = rows[pl.ds(p, 8), :]
+        for i in range(5):
+            n = min(128, WIDTH - 128 * i)
+            kbf[t, :, i * 128 : i * 128 + n] = dst[pl.ds(i, CAP, stride=PITCH), 0:n].astype(BF16)
+        return 0
+
+    keeps = []
+
+    def select_rows(i):
+        lax.fori_loop(8 * i, 8 * i + 8, select, 0)
+        part = pl.ds(8 * i, 8)
+        keeps.append(pltpu.make_async_copy(kbf.at[part], kg.at[part], ksem.at[i]))
+        keeps[-1].start()
+
+    for i in range(4):
+        turn_rows(i)
     next(quick)
-    turn_rows(1)
+    for i in range(4, 8):
+        turn_rows(i)
+    for cp in places:
+        cp.wait_recv()
+    own_pos.wait()
+    to_smem = pltpu.make_async_copy(posv, poss, lsem.at[0])
+    to_smem.start()
+    keep_pos = pltpu.make_async_copy(posv, pall, lsem.at[2])
+    keep_pos.start()
     next(quick)
-    turn_rows(2)
+    next(big)
+    to_smem.wait()
+    next(quick)
+    select_rows(0)
     next(quick)
     next(quick)
     next(quick)
-    turn_rows(3)
-    next(quick)
-    next(big)
-    turn_rows(4)
+    select_rows(1)
     for _ in quick:
         pass
+    next(big)
 
     def widen(i, _):
         xa[pl.ds(pl.multiple_of(i * 256, 256), 256), :] = agbuf[i].reshape(256, 128).astype(F32)
@@ -195,10 +222,12 @@
     lax.fori_loop(0, 16, widen, 0)
 
     def lay(k, _):
-        xown[:, pl.ds(pl.multiple_of(k * 128, 128), 128)] = xa[pl.ds(64 + k, 32, stride=128), :].astype(BF16)
-        return 0
-
-    lax.fori_loop(0, CHUNKS + 1, lay, 0)
+        for u in range(3):
+            cols = pl.ds(pl.multiple_of(k * 384 + u * 128, 128), 128)
+            xown[:, cols] = xa[pl.ds(64 + 3 * k + u, 32, stride=128), :].astype(BF16)
+        return 0
+
+    lax.fori_loop(0, (CHUNKS + 1) // 3, lay, 0)
     zpost = Post(zss, zrs)
     up, down, over = (at.grp(1), at.c), (at.grp(-1), at.c), (at.grp(0, True), at.c)
     own_x = pltpu.make_async_copy(xown, xall.at[at.g], lsem.at[4])
@@ -206,24 +235,15 @@
     z_up = zpost.send(xown, xall.at[at.g], up)
     z_down = zpost.send(xown, xall.at[at.g], down)
     z_over = [zpost.send(xown, xall.at[at.g], over)]
-    for cp in places:
-        cp.wait_recv()
-    own_pos.wait()
-    to_smem = pltpu.make_async_copy(posv, poss, lsem.at[0])
-    to_smem.start()
-    keep_pos = pltpu.make_async_copy(posv, pall, lsem.at[2])
-    keep_pos.start()
-
     def lay_q(j, _):
-        qbuf[pl.ds(pl.multiple_of(j * 32, 32), 32), :] = xa[pl.ds(j, 32, stride=128), :].astype(BF16)
-        return 0
-
-    lax.fori_loop(0, IHEADS, lay_q, 0)
+        for u in range(4):
+            qbuf[pl.ds(pl.multiple_of(j * 128 + u * 32, 32), 32), :] = xa[pl.ds(4 * j + u, 32, stride=128), :].astype(BF16)
+        return 0
+
+    lax.fori_loop(0, IHEADS // 4, lay_q, 0)
     wt[...] = jnp.concatenate([xa[pl.ds(121, 32, stride=128), :], jnp.zeros((96, 128), F32)], axis=0).T
-    w = jnp.concatenate([wt[pl.ds(u, 16, stride=4), 0:32] for u in range(4)], axis=1)
-    turn_rows(5)
-    turn_rows(6)
-    turn_rows(7)
+    wq[...] = jnp.concatenate([wt[pl.ds(u, 16, stride=4), 0:32] for u in range(4)], axis=1)
+    select_rows(2)
     next(big)
     load_keys.wait()
 
@@ -235,7 +255,7 @@
                 k, qbuf[i * 256 : i * 256 + 256, :], (((1,), (1,)), ((), ())), preferred_element_type=F32
             )
             for u in (0, 1):
-                t = jnp.maximum(p[:, u * 128 : u * 128 + 128], 0.0) * w[2 * i + u : 2 * i + u + 1, :]
+                t = jnp.maximum(p[:, u * 128 : u * 128 + 128], 0.0) * wq[2 * i + u : 2 * i + u + 1, :]
                 a = t if a is None else a + t
         a = a + pltpu.roll(a, 64, 1)
         a = (a + pltpu.roll(a, 32, 1)).T
@@ -252,7 +272,6 @@
     index(0)
     next(big)
     index(1)
-    next(big)
     z_up.wait_recv()
     low = xall.at[at.grp(-1)]
     z_low = zpost.send(low.at[pl.ds(0, 16)], low.at[pl.ds(0, 16)], up)
@@ -261,43 +280,15 @@
     high_x = xall.at[at.grp(1)]
     z_high = zpost.send(high_x.at[pl.ds(16, 16)], high_x.at[pl.ds(16, 16)], down)
     z_over.append(zpost.send(high_x, high_x, over))
+    next(big)
     index(2)
     next(big)
-    index(3)
-    next(big)
-    to_smem.wait()
-
-    def select(t, _):
-        c, line = t // 2, lax.rem(t, 2) * 2
-
-        def pick(j, _):
-            for u in range(64):
-                p = poss[c, line + j // 2, lax.rem(j, 2) * 64 + u]
-                dst[pl.ds((j * 64 + u) * PITCH, 8), :] = rows[pl.ds(p, 8), :]
-            return 0
-
-        lax.fori_loop(0, CAP // 64, pick, 0)
-        for i in range(5):
-            n = min(128, WIDTH - 128 * i)
-            kbf[t, :, i * 128 : i * 128 + n] = dst[pl.ds(i, CAP, stride=PITCH), 0:n].astype(BF16)
-        return 0
-
-    keeps = []
-
-    def select_rows(i):
-        lax.fori_loop(8 * i, 8 * i + 8, select, 0)
-        part = pl.ds(8 * i, 8)
-        keeps.append(pltpu.make_async_copy(kbf.at[part], kg.at[part], ksem.at[i]))
-        keeps[-1].start()
-
-    select_rows(0)
+    select_rows(3)
     z_low.wait_recv()
     z_high.wait_recv()
     far = xall.at[at.grp(2)]
     z_over.append(zpost.send(far, far, over))
-    select_rows(1)
-    select_rows(2)
-    select_rows(3)
+    index(3)
     for _ in big:
         pass
     for cp in z_over:
@@ -330,6 +321,7 @@
             VMEM((32, TOKW), BF16),
             VMEM((IHEADS * 32, 128), BF16),
             VMEM((128, 128), F32),
+            VMEM((16, 128), F32),
             VMEM((WIDTH, CACHE), BF16),
             VMEM((CACHE * PITCH + 8, 128), F32),
             VMEM((CAP * PITCH + 8, 128), F32),
@@ -470,9 +462,7 @@
 ):
     at = Place()
     near = {}
-    for dx, dy in [(2, 2), (0, 2), (1, 2), (3, 2), (2, 0), (2, 1), (2, 3)] + [
-        (dx, dy) for dx in (0, 1, 3) for dy in (0, 1, 3)
-    ]:
+    def fetch(dx, dy):
         i = at.ctx(0, dx, dy)
         n = len(near)
         pair = pl.ds(2 * i, 2)
@@ -483,6 +473,9 @@
         for cp in near[dx, dy]:
             cp.start()
 
+    for dx, dy in [(2, 2), (0, 2), (1, 2), (3, 2), (2, 0), (2, 1), (2, 3)]:
+        fetch(dx, dy)
+
     def work(h, d):
         for e in range(4):
             for cp in near.pop((e, d % 4) if h == 0 else (d % 4, e), ()):
@@ -496,6 +489,8 @@
     load_dn = pltpu.make_async_copy(dn, dnbuf, lsem.at[5])
     for cp in loads + [load_dn]:
         cp.start()
+    for dx, dy in [(dx, dy) for dx in (1, 3, 0) for dy in (1, 3, 0)]:
+        fetch(dx, dy)
     at.greet()
     post = Post(ss, rs)
     flow = plane_scatter(post, at, work, o, l, (r1, l1, m1, ml1, r2, l2, p1, pl1, r3, l3, m2, ml2, r4, l4), attn)
@@ -513,7 +508,6 @@
         return 0
 
     lax.fori_loop(0, MODEL // 1024, expand, 0)
-    next(flow)
     gates = xbuf[:, :, MODEL:TOKW].reshape(256, 128).astype(F32)
     lane = lax.broadcasted_iota(jnp.int32, (256, 128), 1)
     for e in (0, 1):
@@ -534,34 +528,34 @@
     order = (2, 1, -1, 0)
     swaps = [zpost.send(mp.at[at.grp(d, True)], rc.at[i], over) for i, d in enumerate(order)]
     next(flow)
-    next(flow)
 
     def add(i, d):
         swaps[i].wait_recv()
         b = at.grp(d)
         mp[b] = (mp[b].astype(F32) + rc[i].astype(F32)).astype(BF16)
-
-    add(0, 2)
-    far = mp.at[at.grp(2)]
-    za = zpost.send(far.at[pl.ds(0, 16)], rz1.at[0], zup)
-    zb = zpost.send(far.at[pl.ds(16, 16)], rz1.at[1], zdown)
+        return mp.at[b]
+
+    low, top = pl.ds(0, 16), pl.ds(16, 16)
+    far = add(0, 2)
+    za = zpost.send(far.at[low], rz1.at[0], zup)
+    zb = zpost.send(far.at[top], rz1.at[1], zdown)
+    above = add(1, 1)
+    zc = [zpost.send(above.at[top], rz2.at[0, top], zup)]
+    below = add(2, -1)
+    zd = [zpost.send(below.at[low], rz2.at[1, low], zdown)]
     next(flow)
-    add(1, 1)
-    add(2, -1)
     next(flow)
     za.wait_recv()
-    b = at.grp(1)
-    mp[b, 0:16] = (mp[b, 0:16].astype(F32) + rz1[0].astype(F32)).astype(BF16)
-    zc = zpost.send(mp.at[b], rz2.at[0], zup)
+    above[0:16] = (above[0:16].astype(F32) + rz1[0].astype(F32)).astype(BF16)
+    zc.append(zpost.send(above.at[low], rz2.at[0, low], zup))
     zb.wait_recv()
-    b2 = at.grp(-1)
-    mp[b2, 16:32] = (mp[b2, 16:32].astype(F32) + rz1[1].astype(F32)).astype(BF16)
-    zd = zpost.send(mp.at[b2], rz2.at[1], zdown)
+    below[16:32] = (below[16:32].astype(F32) + rz1[1].astype(F32)).astype(BF16)
+    zd.append(zpost.send(below.at[top], rz2.at[1, top], zdown))
     swaps[3].wait_recv()
-    next(flow)
-    next(flow)
-    zc.wait_recv()
-    zd.wait_recv()
+    for _ in range(5):
+        next(flow)
+    for cp in zc + zd:
+        cp.wait_recv()
 
     def spread(k, _):
         cols = pl.ds(pl.multiple_of(k * 128, 128), 128)
@@ -632,8 +626,8 @@
             dma((6,)),
             dma((64,)),
             dma((64,)),
-            dma((23,)),
-            dma((23,)),
+            dma((25,)),
+            dma((25,)),
         ],
         compiler_params=pltpu.CompilerParams(collective_id=1, has_side_effects=True, vmem_limit_bytes=58 * 2**20),
     )(*args)

time: 136 us -> 114 us (0.84)
  Pallas kernels: 131 us -> 109 us
    pallas_call x1, Pallas kernels: 79 us -> 62.5 us  [gather_all(): pl.pallas_call(gather_kernel, out_shape=(jax.ShapeDtypeStruct((16, 2, WID...]
    pallas_call x1, Pallas kernels: 52.2 us -> 46.4 us  [reduce_all(): pl.pallas_call(reduce_kernel, out_shape=(jax.ShapeDtypeStruct((2, HEADS,...]
where the time goes in v3:
time: 114 us
  Pallas kernels  109 us (96%)
  local copies, waits for them, and re-layouts  4.02 us (4%)
    pallas_call x1, Pallas kernels, gather_all(): pl.pallas_call(gather_kernel, out_shape=(jax.ShapeDtypeStruct((16, 2, WID...  62.5 us
    pallas_call x1, Pallas kernels, reduce_all(): pl.pallas_call(reduce_kernel, out_shape=(jax.ShapeDtypeStruct((2, HEADS,...  46.4 us
    unnamed x5, local copies, waits for them, and re-layouts  4.02 us

profile of v3, /device:TPU:0, one launch (start us, length us, event | category | flops | bytes accessed | tf_op | source)
XLA Modules:
  0.0 113.6 jit_solution(1169012714146248292)
XLA Ops:
  0.6 62.5 %shard_map.157 = (bf16[16,2,576,128]{3,2,1,0:T(8,128)(2,1)}, s32[16,8,128]{2,1,0:T(8,128)}, bf16[8,32,7296]{2,1,0:T(8,128)(2,1)}, bf16[32,256,576]{2,1,0:T(8,128)(2,1)}, f32[32,8192]{1,0:T(8,128)}) custom-call(bf16[2,8192]{1,0:T(2,128)(2,1)} %iq.1, bf16[2,64]{1,0:T(2,128)(2,1)} %iw.1, bf16[2,7168]{1,0:T(2,128)(2,1)} %tok.1, s32[2,8]{1,0:T(2,128)} %ids.1, ...), custom_call_target="tpu_custom_call" | custom-call | tf_op jit(solution)/shard_map/pallas_call | solution.py:304
  63.2 0.0 copy-start
  63.2 46.4 %shard_map.158 = (bf16[2,128,512]{2,1,0:T(8,128)(2,1)}, bf16[2,7168]{1,0:T(2,128)(2,1)}) custom-call(s32[16,8,128]{2,1,0:T(8,128)} %get-tuple-element.11.counts, bf16[32,256,576]{2,1,0:T(8,128)(2,1)} %get-tuple-element.12.kg, bf16[16,2,576,128]{3,2,1,0:T(8,128)(2,1)} %get-tuple-element.13.qall, bf16[8,32,7296]{2,1,0:T(8,128)(2,1)} %get-tuple-element.14.xall, ...), custom_call_target="tpu_custom_call" | custom-call | tf_op jit(solution)/shard_map/pallas_call | solution.py:595
  109.6 0.0 copy-done
  109.6 1.0 copy.20
  110.6 1.7 %copy.21 = bf16[2,128,512]{2,1,0:T(8,128)(2,1)} copy(bf16[2,128,512]{2,1,0:T(8,128)(2,1)} %get-tuple-element.21) | data formatting | bytes 524288
  112.3 1.4 %copy.22 = bf16[2,7168]{1,0:T(2,128)(2,1)} copy(bf16[2,7168]{1,0:T(2,128)(2,1)} %get-tuple-element.22) | data formatting | bytes 57344
Async XLA Ops:
  63.2 46.5 %copy-start = (f32[32,8192]{1,0:T(8,128)S(1)}, f32[32,8192]{1,0:T(8,128)}, u32[]{:S(2)}) copy-start(f32[32,8192]{1,0:T(8,128)} %get-tuple-element.20) | copy-start | bytes 3145732

commit v4 on v3

--- a/solution.py
+++ b/solution.py
@@ -67,9 +67,10 @@
             cp.wait_send()
 
 
-def plane_gather(post, at, part):
-    def both(ref, axis):
-        return post.send(ref, ref, at.near(axis, 1)), post.send(ref, ref, at.near(axis, -1))
+def plane_gather(post, at, own, part):
+    def both(ref, axis, src=None):
+        src = ref if src is None else src
+        return post.send(src, ref, at.near(axis, 1)), post.send(src, ref, at.near(axis, -1))
 
     def split(src, h, axis, plus, minus):
         plus.wait_recv()
@@ -79,8 +80,8 @@
         hi = part(src(1), h, 1)
         return a, post.send(hi, hi, at.near(axis, -1))
 
-    first = [both(part(at.c, h, None), h) for h in (0, 1)]
-    across = {(h, 0): both(part(at.c, h, None), 1 - h) for h in (0, 1)}
+    first = [both(part(at.c, h, None), h, own.at[h]) for h in (0, 1)]
+    across = {(h, 0): both(part(at.c, h, None), 1 - h, own.at[h]) for h in (0, 1)}
     yield
     second = []
     for h in (0, 1):
@@ -142,15 +143,16 @@
         pst[o, 5:8, :] = jnp.zeros((3, 128), jnp.int32)
     at.greet()
     few = Post(kss, krs)
-    quick = plane_gather(few, at, lambda i, h, q: agbuf.at[i, h] if q is None else agbuf.at[i, h, pl.ds(64 * q, 64)])
+    quick = plane_gather(
+        few, at, agbuf.at[at.c], lambda i, h, q: agbuf.at[i, h] if q is None else agbuf.at[i, h, pl.ds(64 * q, 64)]
+    )
     next(quick)
     places = [few.send(pst.at[at.peer(k)[1]], posv.at[at.c], at.peer(k)) for k in range(1, 16)]
     own_pos = pltpu.make_async_copy(pst.at[at.c], posv.at[at.c], lsem.at[2])
     own_pos.start()
-    own_q.wait()
     many = Post(ss, rs)
     big = plane_gather(
-        many, at, lambda i, h, q: qall.at[i, h] if q is None else qall.at[i, h, pl.ds(HALF * q, HALF)]
+        many, at, aq, lambda i, h, q: qall.at[i, h] if q is None else qall.at[i, h, pl.ds(HALF * q, HALF)]
     )
     next(big)
 
@@ -293,7 +295,7 @@
         pass
     for cp in z_over:
         cp.wait_recv()
-    for cp in keeps + [own_x, keep_pos]:
+    for cp in keeps + [own_x, keep_pos, own_q]:
         cp.wait()
     for post in (few, many, zpost):
         post.finish()
@@ -310,7 +312,7 @@
             jax.ShapeDtypeStruct((32, CAP, WIDTH), BF16),
             jax.ShapeDtypeStruct((32, CACHE), F32),
         ),
-        in_specs=[pl.BlockSpec(memory_space=VMEM)] * 8 + [pl.BlockSpec(memory_space=ANY)] * 3,
+        in_specs=[pl.BlockSpec(memory_space=VMEM)] * 9 + [pl.BlockSpec(memory_space=ANY)] * 2,
         out_specs=(pl.BlockSpec(memory_space=ANY),) * 4 + (pl.BlockSpec(memory_space=VMEM),),
         scratch_shapes=[
             VMEM((256, 128), F32),

time: 114 us -> 109 us (0.956)
  Pallas kernels: 109 us -> 104 us
    pallas_call x1, Pallas kernels: 62.5 us -> 57 us  [gather_all(): pl.pallas_call(gather_kernel, out_shape=(jax.ShapeDtypeStruct((16, 2, WID...]
where the time goes in v4:
time: 109 us
  Pallas kernels  104 us (95%)
  local copies, waits for them, and re-layouts  4.02 us (4%)
    pallas_call x1, Pallas kernels, gather_all(): pl.pallas_call(gather_kernel, out_shape=(jax.ShapeDtypeStruct((16, 2, WID...  57 us
    pallas_call x1, Pallas kernels, reduce_all(): pl.pallas_call(reduce_kernel, out_shape=(jax.ShapeDtypeStruct((2, HEADS,...  47.4 us
    unnamed x5, local copies, waits for them, and re-layouts  4.02 us

profile of v4, /device:TPU:0, one launch (start us, length us, event | category | flops | bytes accessed | tf_op | source)
XLA Modules:
  0.0 109.1 jit_solution(9873647538397720725)
XLA Ops:
  0.6 57.0 %shard_map.157 = (bf16[16,2,576,128]{3,2,1,0:T(8,128)(2,1)}, s32[16,8,128]{2,1,0:T(8,128)}, bf16[8,32,7296]{2,1,0:T(8,128)(2,1)}, bf16[32,256,576]{2,1,0:T(8,128)(2,1)}, f32[32,8192]{1,0:T(8,128)}) custom-call(bf16[2,8192]{1,0:T(2,128)(2,1)} %iq.1, bf16[2,64]{1,0:T(2,128)(2,1)} %iw.1, bf16[2,7168]{1,0:T(2,128)(2,1)} %tok.1, s32[2,8]{1,0:T(2,128)} %ids.1, ...), custom_call_target="tpu_custom_call" | custom-call | tf_op jit(solution)/shard_map/pallas_call | solution.py:306
  57.6 0.0 copy-start
  57.7 47.4 %shard_map.158 = (bf16[2,128,512]{2,1,0:T(8,128)(2,1)}, bf16[2,7168]{1,0:T(2,128)(2,1)}) custom-call(s32[16,8,128]{2,1,0:T(8,128)} %get-tuple-element.11.counts, bf16[32,256,576]{2,1,0:T(8,128)(2,1)} %get-tuple-element.12.kg, bf16[16,2,576,128]{3,2,1,0:T(8,128)(2,1)} %get-tuple-element.13.qall, bf16[8,32,7296]{2,1,0:T(8,128)(2,1)} %get-tuple-element.14.xall, ...), custom_call_target="tpu_custom_call" | custom-call | tf_op jit(solution)/shard_map/pallas_call | solution.py:597
  105.0 0.0 copy-done
  105.0 1.0 copy.20
  106.0 1.7 %copy.21 = bf16[2,128,512]{2,1,0:T(8,128)(2,1)} copy(bf16[2,128,512]{2,1,0:T(8,128)(2,1)} %get-tuple-element.21) | data formatting | bytes 524288
  107.7 1.4 %copy.22 = bf16[2,7168]{1,0:T(2,128)(2,1)} copy(bf16[2,7168]{1,0:T(2,128)(2,1)} %get-tuple-element.22) | data formatting | bytes 57344
Async XLA Ops:
  57.6 47.4 %copy-start = (f32[32,8192]{1,0:T(8,128)S(1)}, f32[32,8192]{1,0:T(8,128)}, u32[]{:S(2)}) copy-start(f32[32,8192]{1,0:T(8,128)} %get-tuple-element.20) | copy-start | bytes 3145732

commit v5 on v4

--- a/solution.py
+++ b/solution.py
@@ -212,10 +212,8 @@
     next(quick)
     next(quick)
     next(quick)
-    select_rows(1)
     for _ in quick:
         pass
-    next(big)
 
     def widen(i, _):
         xa[pl.ds(pl.multiple_of(i * 256, 256), 256), :] = agbuf[i].reshape(256, 128).astype(F32)
@@ -245,6 +243,8 @@
     lax.fori_loop(0, IHEADS // 4, lay_q, 0)
     wt[...] = jnp.concatenate([xa[pl.ds(121, 32, stride=128), :], jnp.zeros((96, 128), F32)], axis=0).T
     wq[...] = jnp.concatenate([wt[pl.ds(u, 16, stride=4), 0:32] for u in range(4)], axis=1)
+    next(big)
+    select_rows(1)
     select_rows(2)
     next(big)
     load_keys.wait()
@@ -406,7 +406,7 @@
             d = 0 if e >= 2 else 1
             i = at.ctx(a, 1 - 2 * d, e)
             s2[h, d, e] = both(o.at[i, h], l.at[i, h], r2.at[h, d, e], l2.at[h, d, e], at.near(a, 1 - 2 * d))
-    yield
+        yield
     for e in (0, 2, 1, 3):
         for h in (0, 1):
             a = 1 - h
@@ -541,6 +541,7 @@
     far = add(0, 2)
     za = zpost.send(far.at[low], rz1.at[0], zup)
     zb = zpost.send(far.at[top], rz1.at[1], zdown)
+    next(flow)
     above = add(1, 1)
     zc = [zpost.send(above.at[top], rz2.at[0, top], zup)]
     below = add(2, -1)

time: 109 us -> 111 us (1.018)
  Pallas kernels: 104 us -> 106 us
    pallas_call x1, Pallas kernels: 47.4 us -> 48.6 us  [reduce_all(): pl.pallas_call(reduce_kernel, out_shape=(jax.ShapeDtypeStruct((2, HEADS,...]
where the time goes in v5:
time: 111 us
  Pallas kernels  106 us (95%)
  local copies, waits for them, and re-layouts  4.02 us (4%)
    pallas_call x1, Pallas kernels, gather_all(): pl.pallas_call(gather_kernel, out_shape=(jax.ShapeDtypeStruct((16, 2, WID...  57.8 us
    pallas_call x1, Pallas kernels, reduce_all(): pl.pallas_call(reduce_kernel, out_shape=(jax.ShapeDtypeStruct((2, HEADS,...  48.6 us
    unnamed x5, local copies, waits for them, and re-layouts  4.02 us

profile of v5, /device:TPU:0, one launch (start us, length us, event | category | flops | bytes accessed | tf_op | source)
XLA Modules:
  0.0 111.1 jit_solution(3621685391471900085)
XLA Ops:
  0.6 57.8 %shard_map.157 = (bf16[16,2,576,128]{3,2,1,0:T(8,128)(2,1)}, s32[16,8,128]{2,1,0:T(8,128)}, bf16[8,32,7296]{2,1,0:T(8,128)(2,1)}, bf16[32,256,576]{2,1,0:T(8,128)(2,1)}, f32[32,8192]{1,0:T(8,128)}) custom-call(bf16[2,8192]{1,0:T(2,128)(2,1)} %iq.1, bf16[2,64]{1,0:T(2,128)(2,1)} %iw.1, bf16[2,7168]{1,0:T(2,128)(2,1)} %tok.1, s32[2,8]{1,0:T(2,128)} %ids.1, ...), custom_call_target="tpu_custom_call" | custom-call | tf_op jit(solution)/shard_map/pallas_call | solution.py:306
  58.5 0.0 copy-start
  58.5 48.6 %shard_map.158 = (bf16[2,128,512]{2,1,0:T(8,128)(2,1)}, bf16[2,7168]{1,0:T(2,128)(2,1)}) custom-call(s32[16,8,128]{2,1,0:T(8,128)} %get-tuple-element.11.counts, bf16[32,256,576]{2,1,0:T(8,128)(2,1)} %get-tuple-element.12.kg, bf16[16,2,576,128]{3,2,1,0:T(8,128)(2,1)} %get-tuple-element.13.qall, bf16[8,32,7296]{2,1,0:T(8,128)(2,1)} %get-tuple-element.14.xall, ...), custom_call_target="tpu_custom_call" | custom-call | tf_op jit(solution)/shard_map/pallas_call | solution.py:598
  107.1 0.0 copy-done
  107.1 1.0 copy.20
  108.1 1.7 %copy.21 = bf16[2,128,512]{2,1,0:T(8,128)(2,1)} copy(bf16[2,128,512]{2,1,0:T(8,128)(2,1)} %get-tuple-element.21) | data formatting | bytes 524288
  109.8 1.4 %copy.22 = bf16[2,7168]{1,0:T(2,128)(2,1)} copy(bf16[2,7168]{1,0:T(2,128)(2,1)} %get-tuple-element.22) | data formatting | bytes 57344
Async XLA Ops:
  58.5 48.6 %copy-start = (f32[32,8192]{1,0:T(8,128)S(1)}, f32[32,8192]{1,0:T(8,128)}, u32[]{:S(2)}) copy-start(f32[32,8192]{1,0:T(8,128)} %get-tuple-element.20) | copy-start | bytes 3145732
